TPU v7x, 128 devices: a whole 4x4x4 slice. The times are simulated.
128 devices in a mesh: wide: 16 (over x, z), narrow: 8 (over y, core).
Axes of the slice: x: 4, y: 4, z: 4, core: 2. Of those that a mesh axis runs over, the one named last changes fastest.
Arguments:
- leaf_density: bfloat16 [98304, 152], P(('wide', 'narrow')), may hold values from -6 to 6
- m2l_matrices: bfloat16 [189, 152, 152], replicated, may hold values from -0.03125 to 0.03125
- m2m_matrices: bfloat16 [8, 152, 152], replicated, may hold values from -0.15625 to 0.15625
- send_index: int32 [128, 128, 128], P(('wide', 'narrow')), may hold values from 0 to 767
- leaf_source: int32 [189, 98304], P(None, ('wide', 'narrow')), may hold values from -1 to 17151, as said below
- coarse_source: int32 [189, 12288], P(None, ('wide', 'narrow')), may hold values from -1 to 12287, as said below
Outputs:
- leaf_local: float32 [98304, 152], P(('wide', 'narrow'))
- coarse_multipole: bfloat16 [12288, 152], P(('wide', 'narrow'))
- coarse_local: float32 [12288, 152], P(('wide', 'narrow'))
Inputs may be any that keep to these rules, and one draw needn't show every extreme that they name: `leaf_source`: -1 marks an absent source. 0 to 767 is a cell of the target's own device. A larger value 768 + p * 128 + k names slot k of what device p sends to the target's device, where p is another device; for each such pair only a leading run of slots is named, and for every device all 128 slots of some one pair are. `coarse_source`: -1 marks an absent source. Otherwise the source lies in the target's own index of wide or in the one beside it, counting 8 * 96 parent cells to an index of wide.
All inputs are finite; a program needn't handle non-finite values.
Results may differ from a plain program's by a relative error of at most 0.0029.
Values may be sent and summed in bfloat16 or wider, within the bound.
No kernel may reach another device: no remote copies, remote signals or barrier semaphores. Data moves between devices by JAX's collectives and lax.ppermute only.
A program may use at most 128 MiB of HBM per device.

v0:
```python
import math

import jax
import jax.numpy as jnp
from jax import lax
from jax.sharding import PartitionSpec as P


def padded(value, sides, width):
    for axis, dim in sides:
        size, length = (lax.axis_size(axis), value.shape[dim])
        up = [(i, (i + 1) % size) for i in range(size - 1)]
        down = [(j, i) for i, j in up]
        last = lax.slice_in_dim(value, length - width, length, axis=dim)
        leading = lax.slice_in_dim(value, 0, width, axis=dim)
        before = lax.ppermute(last, axis, up)
        after = lax.ppermute(leading, axis, down)
        value = jnp.concatenate([before, value, after], axis=dim)
    return value


def translate(table, index, kmat):
    nblk = index.shape[0] // 27
    targets = index.shape[1]
    width = kmat.shape[1]
    blocks = index.reshape(nblk, 27, targets).transpose(0, 2, 1)
    mats = kmat.reshape(nblk, 27 * width, kmat.shape[2])

    def step(total, pair):
        rows = jnp.take(table, pair[0], axis=0).reshape(targets, 27 * width)
        return (total + jnp.dot(rows, pair[1], preferred_element_type=jnp.float32), None)

    start = jnp.zeros((targets, kmat.shape[2]), jnp.float32)
    total, _ = lax.scan(step, start, (blocks, mats))
    return total


def pick_rows(leaf_density, chosen):
    devices = chosen.shape[0]
    capacity = chosen.shape[1]
    cells = leaf_density.shape[0]
    group = math.gcd(devices, 16)
    blocks = chosen.reshape(devices // group, group * capacity)
    column = jnp.arange(cells, dtype=jnp.int32)[None, :]

    def select(block):
        onehot = (block[:, None] == column).astype(jnp.bfloat16)
        return jnp.dot(onehot, leaf_density, preferred_element_type=jnp.float32).astype(
            jnp.bfloat16
        )

    picked = lax.map(select, blocks)
    return picked.reshape(devices, capacity, leaf_density.shape[1])


def local(leaf_density, m2l_matrices, m2m_matrices, send_index, leaf_source, coarse_source):
    cells = leaf_density.shape[0]
    width = leaf_density.shape[1]
    devices = send_index.shape[1]
    capacity = send_index.shape[2]
    zero_row = jnp.zeros((1, width), jnp.bfloat16)
    outgoing = pick_rows(leaf_density, send_index[0])
    arrived = lax.all_to_all(outgoing, ("wide", "narrow"), split_axis=0, concat_axis=0, tiled=True)
    ghost_rows = arrived.reshape(devices * capacity, width)
    table = jnp.concatenate([leaf_density, ghost_rows, zero_row], axis=0)
    absent = table.shape[0] - 1
    index = jnp.where(leaf_source < 0, absent, leaf_source)
    leaf_local = translate(table, index, m2l_matrices)
    parents = jnp.dot(
        leaf_density.reshape(cells // 8, 8 * width),
        m2m_matrices.reshape(8 * width, width),
        preferred_element_type=jnp.float32,
    ).astype(jnp.bfloat16)
    group = lax.all_gather(parents, "narrow", axis=0, tiled=True)
    group_rows = group.shape[0]
    nearby = padded(group, (("wide", 0),), group_rows)
    table_two = jnp.concatenate([nearby, zero_row], axis=0)
    base = (lax.axis_index("wide") - 1) * group_rows
    cidx = jnp.where(coarse_source < 0, 3 * group_rows, coarse_source - base)
    coarse_local = 0.5 * translate(table_two, cidx, m2l_matrices)
    return (leaf_local, parents, coarse_local)


def solution(mesh):
    placed = (
        P(("wide", "narrow"), None),
        P(),
        P(),
        P(("wide", "narrow"), None, None),
        P(None, ("wide", "narrow")),
        P(None, ("wide", "narrow")),
    )
    return jax.shard_map(
        local,
        mesh=mesh,
        in_specs=placed,
        out_specs=(
            P(("wide", "narrow"), None),
            P(("wide", "narrow"), None),
            P(("wide", "narrow"), None),
        ),
        check_vma=False,
    )
```

profile of v0, /device:TPU:1, one launch (start us, length us, event | category | flops | bytes accessed | tf_op | source)
XLA Modules:
  0.0 962.1 jit_solution(12411048999477643814)
XLA Ops:
  2.6 14.8 %all-gather = bf16[8,96,152]{1,2,0:T(8,128)(2,1)S(1)} all-gather(bf16[1,96,152]{1,2,0:T(8,128)(2,1)S(1)} %bitcast.85), channel_id=1, replica_groups=mesh['wide'=16,'narrow'=8] {'narrow'}, dimensions={0}, use_global_device_ids=true | all-gather | bytes 262656 | tf_op jit(solution)/shard_map/all_gather | solution.py:74
  18.9 4.2 collective-permute-start
  24.0 27.6 %while.33 = (s32[]{:T(128)}, bf16[8,2048,152]{1,2,0:T(8,128)(2,1)}, s32[8,2048]{1,0:T(8,128)S(1)}, bf16[768,152]{0,1:T(8,128)(2,1)}, s32[]{:T(128)}) while((s32[]{:T(128)}, bf16[8,2048,152]{1,2,0:T(8,128)(2,1)}, s32[8,2048]{1,0:T(8,128)S(1)}, bf16[768,152]{0,1:T(8,128)(2,1)}, s32[]{:T(128)}) %tuple.65), condition=%wide.region_1.2_spmd.clone, body=%wide.region_0.1_spmd.clone.sunk | while | flops 480034816 | bytes 880717 | solution.py:52
  24.0 3.4 fusion.36
  27.5 3.4 fusion.36
  30.9 3.5 fusion.36
  34.4 3.4 fusion.36
  37.8 3.5 fusion.36
  41.3 3.4 fusion.36
  44.7 3.4 fusion.36
  48.2 3.4 fusion.36
  51.7 7.4 copy.37
  59.0 8.7 reshape.125
  67.7 7.8 copy.38
  75.5 12.3 %all-to-all-start = ((bf16[128,128,152]{1,2,0:T(8,128)(2,1)}), bf16[128,128,152]{1,2,0:T(8,128)(2,1)}, u32[]{:S(2)}, u32[]{:S(2)}) async-start(bf16[128,128,152]{1,2,0:T(8,128)(2,1)} %copy.38), calls=%async_computation | async-start | bytes 9961472 | tf_op jit(solution)/shard_map/all_to_all | solution.py:63
  88.9 21.2 %copy.40 = bf16[189,152,152]{2,1,0:T(8,128)(2,1)} copy(bf16[189,152,152]{0,2,1:T(8,128)(2,1)} %param.13) | data formatting | bytes 17466624 | tf_op args[1]
  111.1 120.1 %while.35 = (s32[]{:T(128)}, f32[96,152]{0,1:T(8,128)S(1)}, s32[7,96,27]{1,2,0:T(8,128)S(1)}, bf16[2305,152]{1,0:T(8,128)(2,1)S(1)}, bf16[7,4104,152]{2,1,0:T(8,128)(2,1)}, /*index=5*/s32[]{:T(128)}, s32[]{:T(128)}) while((s32[]{:T(128)}, f32[96,152]{0,1:T(8,128)S(1)}, s32[7,96,27]{1,2,0:T(8,128)S(1)}, ...), condition=%wide.region_5.6_spmd.clone, body=%wide.region_4.5_spmd.clone.sunk | while | flops 120220704 | bytes 9703975 | solution.py:34
  111.5 8.4 gather_fusion.1
  125.6 2.7 fusion.42
  128.6 8.4 gather_fusion.1
  145.8 8.4 gather_fusion.1
  162.9 8.4 gather_fusion.1
  180.1 8.4 gather_fusion.1
  197.3 8.4 gather_fusion.1
  214.4 8.4 gather_fusion.1
  231.9 3.0 copy_bitcast_fusion
  234.9 3.7 pad_maximum_fusion
  238.6 9.6 %copy.42 = bf16[17153,152]{1,0:T(8,128)(2,1)} copy(bf16[17153,152]{0,1:T(8,128)(2,1)} %pad_maximum_fusion) | data formatting | bytes 10429024
  248.3 712.6 %while.34 = (s32[]{:T(128)}, f32[768,152]{0,1:T(8,128)S(1)}, s32[7,768,27]{1,2,0:T(8,128)}, bf16[17153,152]{1,0:T(8,128)(2,1)}, bf16[7,4104,152]{2,1,0:T(8,128)(2,1)}, /*index=5*/s32[]{:T(128)}, s32[]{:T(128)}) while((s32[]{:T(128)}, f32[768,152]{0,1:T(8,128)S(1)}, s32[7,768,27]{1,2,0:T(8,128)}, bf16[17153,152]{1,0:T(8,128)(2,1)}, ...), condition=%wide.region_3.4_spmd.clone, body=%wide.region_2.3_spmd.clone.sunk | while | flops 961762560 | bytes 60808804 | solution.py:34
  249.7 52.1 %gather_fusion = bf16[20736,152]{1,0:T(8,128)(2,1)} fusion(bf16[17153,152]{1,0:T(8,128)(2,1)} %get-tuple-element.310, s32[21504]{0:T(1024)S(1)} %pad_clamp_fusion.4), kind=kCustom, calls=%fused_computation.clone.clone.1 | custom fusion | bytes 12690432 | tf_op jit(solution)/shard_map/while/body/eval_jaxpr/jit(_take)/gather | solution.py:30
  301.8 17.2 %reshape.170 = bf16[768,27,152]{2,1,0:T(8,128)(2,1)} reshape(bf16[20736,152]{1,0:T(8,128)(2,1)} %gather_fusion) | data formatting | bytes 12607488 | tf_op jit(solution)/shard_map/while/body/eval_jaxpr/jit(_take)/gather | solution.py:30
  319.0 10.8 %broadcast_select_fusion.4 = bf16[768,27,152]{2,1,0:T(8,128)(2,1)} fusion(bf16[768,27,152]{2,1,0:T(8,128)(2,1)} %reshape.170, pred[768,27]{1,0:T(8,128)(4,1)S(1)} %compare_and_fusion.4), kind=kLoop, calls=%fused_computation.10.clone.1 | loop fusion | flops 3151872 | bytes 12628224 | tf_op jit(solution)/shard_map/while/body/eval_jaxpr/jit(_take)/select_n | solution.py:30
  329.8 15.4 %copy.56 = bf16[768,27,152]{0,2,1:T(8,128)(2,1)} copy(bf16[768,27,152]{2,1,0:T(8,128)(2,1)} %broadcast_select_fusion.4) | data formatting | bytes 12607488 | tf_op jit(solution)/shard_map/while/body/eval_jaxpr/jit(_take)/select_n | solution.py:30
  345.2 4.8 fusion.39
  351.5 52.1 %gather_fusion = bf16[20736,152]{1,0:T(8,128)(2,1)} fusion(bf16[17153,152]{1,0:T(8,128)(2,1)} %get-tuple-element.310, s32[21504]{0:T(1024)S(1)} %pad_clamp_fusion.4), kind=kCustom, calls=%fused_computation.clone.clone.1 | custom fusion | bytes 12690432 | tf_op jit(solution)/shard_map/while/body/eval_jaxpr/jit(_take)/gather | solution.py:30
  403.6 17.2 %reshape.170 = bf16[768,27,152]{2,1,0:T(8,128)(2,1)} reshape(bf16[20736,152]{1,0:T(8,128)(2,1)} %gather_fusion) | data formatting | bytes 12607488 | tf_op jit(solution)/shard_map/while/body/eval_jaxpr/jit(_take)/gather | solution.py:30
  420.9 10.8 %broadcast_select_fusion.4 = bf16[768,27,152]{2,1,0:T(8,128)(2,1)} fusion(bf16[768,27,152]{2,1,0:T(8,128)(2,1)} %reshape.170, pred[768,27]{1,0:T(8,128)(4,1)S(1)} %compare_and_fusion.4), kind=kLoop, calls=%fused_computation.10.clone.1 | loop fusion | flops 3151872 | bytes 12628224 | tf_op jit(solution)/shard_map/while/body/eval_jaxpr/jit(_take)/select_n | solution.py:30
  431.6 15.4 %copy.56 = bf16[768,27,152]{0,2,1:T(8,128)(2,1)} copy(bf16[768,27,152]{2,1,0:T(8,128)(2,1)} %broadcast_select_fusion.4) | data formatting | bytes 12607488 | tf_op jit(solution)/shard_map/while/body/eval_jaxpr/jit(_take)/select_n | solution.py:30
  447.0 4.8 fusion.39
  453.3 52.1 %gather_fusion = bf16[20736,152]{1,0:T(8,128)(2,1)} fusion(bf16[17153,152]{1,0:T(8,128)(2,1)} %get-tuple-element.310, s32[21504]{0:T(1024)S(1)} %pad_clamp_fusion.4), kind=kCustom, calls=%fused_computation.clone.clone.1 | custom fusion | bytes 12690432 | tf_op jit(solution)/shard_map/while/body/eval_jaxpr/jit(_take)/gather | solution.py:30
  505.4 17.2 %reshape.170 = bf16[768,27,152]{2,1,0:T(8,128)(2,1)} reshape(bf16[20736,152]{1,0:T(8,128)(2,1)} %gather_fusion) | data formatting | bytes 12607488 | tf_op jit(solution)/shard_map/while/body/eval_jaxpr/jit(_take)/gather | solution.py:30
  522.7 10.8 %broadcast_select_fusion.4 = bf16[768,27,152]{2,1,0:T(8,128)(2,1)} fusion(bf16[768,27,152]{2,1,0:T(8,128)(2,1)} %reshape.170, pred[768,27]{1,0:T(8,128)(4,1)S(1)} %compare_and_fusion.4), kind=kLoop, calls=%fused_computation.10.clone.1 | loop fusion | flops 3151872 | bytes 12628224 | tf_op jit(solution)/shard_map/while/body/eval_jaxpr/jit(_take)/select_n | solution.py:30
  533.4 15.4 %copy.56 = bf16[768,27,152]{0,2,1:T(8,128)(2,1)} copy(bf16[768,27,152]{2,1,0:T(8,128)(2,1)} %broadcast_select_fusion.4) | data formatting | bytes 12607488 | tf_op jit(solution)/shard_map/while/body/eval_jaxpr/jit(_take)/select_n | solution.py:30
  548.8 4.8 fusion.39
  555.1 52.1 %gather_fusion = bf16[20736,152]{1,0:T(8,128)(2,1)} fusion(bf16[17153,152]{1,0:T(8,128)(2,1)} %get-tuple-element.310, s32[21504]{0:T(1024)S(1)} %pad_clamp_fusion.4), kind=kCustom, calls=%fused_computation.clone.clone.1 | custom fusion | bytes 12690432 | tf_op jit(solution)/shard_map/while/body/eval_jaxpr/jit(_take)/gather | solution.py:30
  607.2 17.2 %reshape.170 = bf16[768,27,152]{2,1,0:T(8,128)(2,1)} reshape(bf16[20736,152]{1,0:T(8,128)(2,1)} %gather_fusion) | data formatting | bytes 12607488 | tf_op jit(solution)/shard_map/while/body/eval_jaxpr/jit(_take)/gather | solution.py:30
  624.5 10.8 %broadcast_select_fusion.4 = bf16[768,27,152]{2,1,0:T(8,128)(2,1)} fusion(bf16[768,27,152]{2,1,0:T(8,128)(2,1)} %reshape.170, pred[768,27]{1,0:T(8,128)(4,1)S(1)} %compare_and_fusion.4), kind=kLoop, calls=%fused_computation.10.clone.1 | loop fusion | flops 3151872 | bytes 12628224 | tf_op jit(solution)/shard_map/while/body/eval_jaxpr/jit(_take)/select_n | solution.py:30
  635.2 15.4 %copy.56 = bf16[768,27,152]{0,2,1:T(8,128)(2,1)} copy(bf16[768,27,152]{2,1,0:T(8,128)(2,1)} %broadcast_select_fusion.4) | data formatting | bytes 12607488 | tf_op jit(solution)/shard_map/while/body/eval_jaxpr/jit(_take)/select_n | solution.py:30
  650.6 4.8 fusion.39
  656.9 52.1 %gather_fusion = bf16[20736,152]{1,0:T(8,128)(2,1)} fusion(bf16[17153,152]{1,0:T(8,128)(2,1)} %get-tuple-element.310, s32[21504]{0:T(1024)S(1)} %pad_clamp_fusion.4), kind=kCustom, calls=%fused_computation.clone.clone.1 | custom fusion | bytes 12690432 | tf_op jit(solution)/shard_map/while/body/eval_jaxpr/jit(_take)/gather | solution.py:30
  709.0 17.2 %reshape.170 = bf16[768,27,152]{2,1,0:T(8,128)(2,1)} reshape(bf16[20736,152]{1,0:T(8,128)(2,1)} %gather_fusion) | data formatting | bytes 12607488 | tf_op jit(solution)/shard_map/while/body/eval_jaxpr/jit(_take)/gather | solution.py:30
  726.3 10.8 %broadcast_select_fusion.4 = bf16[768,27,152]{2,1,0:T(8,128)(2,1)} fusion(bf16[768,27,152]{2,1,0:T(8,128)(2,1)} %reshape.170, pred[768,27]{1,0:T(8,128)(4,1)S(1)} %compare_and_fusion.4), kind=kLoop, calls=%fused_computation.10.clone.1 | loop fusion | flops 3151872 | bytes 12628224 | tf_op jit(solution)/shard_map/while/body/eval_jaxpr/jit(_take)/select_n | solution.py:30
  737.0 15.4 %copy.56 = bf16[768,27,152]{0,2,1:T(8,128)(2,1)} copy(bf16[768,27,152]{2,1,0:T(8,128)(2,1)} %broadcast_select_fusion.4) | data formatting | bytes 12607488 | tf_op jit(solution)/shard_map/while/body/eval_jaxpr/jit(_take)/select_n | solution.py:30
  752.4 4.8 fusion.39
  758.7 52.1 %gather_fusion = bf16[20736,152]{1,0:T(8,128)(2,1)} fusion(bf16[17153,152]{1,0:T(8,128)(2,1)} %get-tuple-element.310, s32[21504]{0:T(1024)S(1)} %pad_clamp_fusion.4), kind=kCustom, calls=%fused_computation.clone.clone.1 | custom fusion | bytes 12690432 | tf_op jit(solution)/shard_map/while/body/eval_jaxpr/jit(_take)/gather | solution.py:30
  810.8 17.2 %reshape.170 = bf16[768,27,152]{2,1,0:T(8,128)(2,1)} reshape(bf16[20736,152]{1,0:T(8,128)(2,1)} %gather_fusion) | data formatting | bytes 12607488 | tf_op jit(solution)/shard_map/while/body/eval_jaxpr/jit(_take)/gather | solution.py:30
  828.1 10.8 %broadcast_select_fusion.4 = bf16[768,27,152]{2,1,0:T(8,128)(2,1)} fusion(bf16[768,27,152]{2,1,0:T(8,128)(2,1)} %reshape.170, pred[768,27]{1,0:T(8,128)(4,1)S(1)} %compare_and_fusion.4), kind=kLoop, calls=%fused_computation.10.clone.1 | loop fusion | flops 3151872 | bytes 12628224 | tf_op jit(solution)/shard_map/while/body/eval_jaxpr/jit(_take)/select_n | solution.py:30
  838.9 15.4 %copy.56 = bf16[768,27,152]{0,2,1:T(8,128)(2,1)} copy(bf16[768,27,152]{2,1,0:T(8,128)(2,1)} %broadcast_select_fusion.4) | data formatting | bytes 12607488 | tf_op jit(solution)/shard_map/while/body/eval_jaxpr/jit(_take)/select_n | solution.py:30
  854.2 4.8 fusion.39
  860.5 52.1 %gather_fusion = bf16[20736,152]{1,0:T(8,128)(2,1)} fusion(bf16[17153,152]{1,0:T(8,128)(2,1)} %get-tuple-element.310, s32[21504]{0:T(1024)S(1)} %pad_clamp_fusion.4), kind=kCustom, calls=%fused_computation.clone.clone.1 | custom fusion | bytes 12690432 | tf_op jit(solution)/shard_map/while/body/eval_jaxpr/jit(_take)/gather | solution.py:30
  912.6 17.2 %reshape.170 = bf16[768,27,152]{2,1,0:T(8,128)(2,1)} reshape(bf16[20736,152]{1,0:T(8,128)(2,1)} %gather_fusion) | data formatting | bytes 12607488 | tf_op jit(solution)/shard_map/while/body/eval_jaxpr/jit(_take)/gather | solution.py:30
  929.9 10.8 %broadcast_select_fusion.4 = bf16[768,27,152]{2,1,0:T(8,128)(2,1)} fusion(bf16[768,27,152]{2,1,0:T(8,128)(2,1)} %reshape.170, pred[768,27]{1,0:T(8,128)(4,1)S(1)} %compare_and_fusion.4), kind=kLoop, calls=%fused_computation.10.clone.1 | loop fusion | flops 3151872 | bytes 12628224 | tf_op jit(solution)/shard_map/while/body/eval_jaxpr/jit(_take)/select_n | solution.py:30
  940.7 15.4 %copy.56 = bf16[768,27,152]{0,2,1:T(8,128)(2,1)} copy(bf16[768,27,152]{2,1,0:T(8,128)(2,1)} %broadcast_select_fusion.4) | data formatting | bytes 12607488 | tf_op jit(solution)/shard_map/while/body/eval_jaxpr/jit(_take)/select_n | solution.py:30
  956.0 4.8 fusion.39
  (156 shorter events, 77.0 us)
Async XLA Ops:
  0.6 1.6 copy-start
  2.6 14.8 %copy-start.4 = (bf16[96,152]{0,1:T(8,128)(2,1)}, bf16[96,152]{0,1:T(8,128)(2,1)S(1)}, u32[]{:S(2)}) copy-start(bf16[96,152]{0,1:T(8,128)(2,1)S(1)} %convolution_convert_fusion) | copy-start | bytes 87556
  17.6 92.5 %collective-permute-start.1 = (bf16[768,152]{0,1:T(8,128)(2,1)S(1)}, bf16[768,152]{0,1:T(8,128)(2,1)S(1)}, u32[]{:S(2)}, u32[]{:S(2)}) collective-permute-start(bf16[768,152]{0,1:T(8,128)(2,1)S(1)} %reshape.150), channel_id=1, source_target_pairs={{8,0},{16,8},{24,16},{32,24},{40,32},{48,40},{56,48},{64,56},{72,6... | collective-permute-start | bytes 700424 | tf_op jit(solution)/shard_map/ppermute | solution.py:17
  18.9 91.2 %collective-permute-start = (bf16[768,152]{0,1:T(8,128)(2,1)S(1)}, bf16[768,152]{0,1:T(8,128)(2,1)S(1)}, u32[]{:S(2)}, u32[]{:S(2)}) collective-permute-start(bf16[768,152]{0,1:T(8,128)(2,1)S(1)} %reshape.150), channel_id=1, source_target_pairs={{0,8},{8,16},{16,24},{24,32},{32,40},{40,48},{48,56},{56,64},{64,7... | collective-permute-start | bytes 700424 | tf_op jit(solution)/shard_map/ppermute | solution.py:16
  75.5 12.4 %copy-start.3 = (s32[189,768]{1,0:T(8,128)S(1)}, s32[189,768]{1,0:T(8,128)}, u32[]{:S(2)}) copy-start(s32[189,768]{1,0:T(8,128)} %param.16) | copy-start | bytes 1741828
  75.5 156.4 %all-to-all-start = ((bf16[128,128,152]{1,2,0:T(8,128)(2,1)}), bf16[128,128,152]{1,2,0:T(8,128)(2,1)}, u32[]{:S(2)}, u32[]{:S(2)}) async-start(bf16[128,128,152]{1,2,0:T(8,128)(2,1)} %copy.38), calls=%async_computation | async-start | bytes 9961472 | tf_op jit(solution)/shard_map/all_to_all | solution.py:63
  88.9 21.2 %copy-start.5 = (s32[189,96]{1,0:T(8,128)S(1)}, s32[189,96]{1,0:T(8,128)}, u32[]{:S(2)}) copy-start(s32[189,96]{1,0:T(8,128)} %param.17) | copy-start | bytes 217732
  231.9 3.0 copy-start.2
  238.6 9.6 %copy-start.6 = (f32[768,152]{0,1:T(8,128)S(1)}, f32[768,152]{0,1:T(8,128)}, u32[]{:S(2)}) copy-start(f32[768,152]{0,1:T(8,128)} %custom-call) | copy-start | bytes 1400836
  960.9 0.8 copy-start.7
  960.9 1.2 copy-start.1
where the time goes:
time: 971 us; the launch traced here: 962 us
  local copies, waits for them, and re-layouts  754 us (78%)
  other arithmetic  93.5 us (10%)
  matrix products  80.4 us (8%)
  starting transfers between devices  17.8 us (2%)
  blocking collectives  14.8 us (2%)
    gather x28, local copies, waits for them, and re-layouts, step(): rows = jnp.take(table, pair[0], axis=0).reshape(targets, 27 * width)  554 us
    select_n x28, local copies, waits for them, and re-layouts, step(): rows = jnp.take(table, pair[0], axis=0).reshape(targets, 27 * width)  128 us
    select_n x28, other arithmetic, step(): rows = jnp.take(table, pair[0], axis=0).reshape(targets, 27 * width)  87.9 us
    dot_general x14, matrix products, step(): jnp.dot(rows, pair[1], preferred_element_type=jnp.float32)  52.5 us
    unnamed x21, local copies, waits for them, and re-layouts  34.4 us
    dot_general x8, matrix products, select(): jnp.dot(onehot, leaf_density, preferred_element_type=jnp.float32)  27.5 us
  transfers between devices with their start and end apart: 3, of which 0 were waited for; matrix products, arithmetic and copies ran while one was open for 20% of the time, Pallas kernels for 0%

commit v1 on v0

v1 whole, which is shorter than its diff:
```python
import functools

import jax, jax.numpy as jnp
from jax import lax
from jax.experimental import pallas as pl
from jax.experimental.pallas import tpu as pltpu
from jax.sharding import PartitionSpec as P

LANES = 128


def translate_kernel(leaves, tail, idx_hbm, m2l_ref, leaf_ref, far_ref, near_ref, out_leaf, out_coarse,
                     table, acc, idx_vmem, f0, f1, f2, w0, w1, w2, s0, s1, s2, sem, vsem):
    step = pl.program_id(0)
    steps = pl.num_programs(0)
    rows_f = (f0, f1, f2)
    mats = (w0, w1, w2)
    smem = (s0, s1, s2)
    count = leaves + tail
    width = m2l_ref.shape[1]

    def fetch(k, s):
        return pltpu.make_async_copy(idx_vmem.at[3 * s + k], smem[k], sem.at[k])

    def gather(k):
        for t in range(count):
            i = smem[k][t // LANES, t % LANES]
            rows_f[k][pl.ds(2 * t, 2), :] = table[pl.ds(i, 2), :]

    def multiply(k):
        low = rows_f[k][pl.ds(0, count, stride=2), :].astype(jnp.bfloat16)
        high = rows_f[k][pl.ds(1, count, stride=2), :].astype(jnp.bfloat16)
        acc[...] += jnp.dot(jnp.concatenate([low, high], axis=1), mats[k][...], preferred_element_type=jnp.float32)

    def load_matrix(k):
        mats[k][0:width, 0:width] = m2l_ref[k]

    @pl.when(step == 0)
    def _():
        copy = pltpu.make_async_copy(idx_hbm, idx_vmem, vsem)
        copy.start()
        acc[...] = jnp.zeros_like(acc)
        f2[...] = jnp.zeros_like(f2)
        for w in mats:
            w[...] = jnp.zeros_like(w)
        table[0:8, :] = jnp.zeros((8, LANES), jnp.float32)
        place = 8
        for ref in (leaf_ref, far_ref, near_ref):
            n = ref.shape[0]
            block = 256
            start = place

            @pl.loop(0, n // block)
            def _(b):
                src = pl.ds(pl.multiple_of(b * block, block), block)
                dst = pl.ds(pl.multiple_of(start + b * block, 8), block)
                table[dst, :] = ref[src, :].astype(jnp.float32)
            place += n
        copy.wait()
        for k in range(3):
            fetch(k, 0).start()

    fetch(0, step).wait()
    gather(0)
    multiply(2)

    @pl.when(step + 1 < steps)
    def _():
        fetch(0, step + 1).start()
    for k in range(3):
        load_matrix(k)
    fetch(1, step).wait()
    gather(1)
    multiply(0)

    @pl.when(step + 1 < steps)
    def _():
        fetch(1, step + 1).start()
    fetch(2, step).wait()
    gather(2)
    multiply(1)

    @pl.when(step + 1 < steps)
    def _():
        fetch(2, step + 1).start()

    @pl.when(step == steps - 1)
    def _():
        multiply(2)
        out_leaf[...] = acc[0:leaves, 0:width]
        out_coarse[...] = 0.5 * acc[leaves:count, 0:width]


def translate(idx, m2l, leaf2, far2, near2, leaves, tail):
    noff, width, _ = m2l.shape
    count = leaves + tail
    whole = lambda ref: pl.BlockSpec(ref.shape, lambda s: (0,) * ref.ndim, pipeline_mode=pl.Buffered(1))
    rows = 8 + leaf2.shape[0] + far2.shape[0] + near2.shape[0]
    return pl.pallas_call(
        functools.partial(translate_kernel, leaves, tail),
        grid=(noff // 3,),
        in_specs=[
            pl.BlockSpec(memory_space=pl.ANY),
            pl.BlockSpec((3, width, width), lambda s: (s, 0, 0)),
            whole(leaf2), whole(far2), whole(near2),
        ],
        out_specs=[
            pl.BlockSpec((leaves, width), lambda s: (0, 0)),
            pl.BlockSpec((tail, width), lambda s: (0, 0)),
        ],
        out_shape=[
            jax.ShapeDtypeStruct((leaves, width), jnp.float32),
            jax.ShapeDtypeStruct((tail, width), jnp.float32),
        ],
        scratch_shapes=[
            pltpu.VMEM((rows, LANES), jnp.float32),
            pltpu.VMEM((count, 2 * LANES), jnp.float32),
            pltpu.VMEM(idx.shape, jnp.int32),
        ] + [pltpu.VMEM((2 * count, LANES), jnp.float32)] * 3
        + [pltpu.VMEM((2 * LANES, 2 * LANES), jnp.bfloat16)] * 3
        + [pltpu.SMEM(idx.shape[1:], jnp.int32)] * 3
        + [pltpu.SemaphoreType.DMA((3,)), pltpu.SemaphoreType.DMA],
        compiler_params=pltpu.CompilerParams(vmem_limit_bytes=58 * 2**20),
        cost_estimate=pl.CostEstimate(flops=2 * noff * count * width * width, bytes_accessed=20 * 2**20, transcendentals=0),
    )(idx, m2l, leaf2, far2, near2)


def pick_kernel(block, idx_ref, cells_ref, out_ref, table, rows_f):
    @pl.when(pl.program_id(0) == 0)
    def _():
        table[...] = cells_ref[...].astype(jnp.float32)

    @pl.loop(0, block // LANES)
    def _(r):
        row = idx_ref.at[pl.program_id(0) * (block // LANES) + r]
        base = pl.multiple_of(r * 2 * LANES, 2 * LANES)
        for u in range(LANES):
            rows_f[pl.ds(2 * u, 2), :] = table[pl.ds(row[u], 2), :]
        out_ref[pl.ds(base, 2 * LANES), :] = rows_f[...].astype(jnp.bfloat16)


def pick_rows(leaf2, chosen):
    devices, capacity = chosen.shape
    block = 16 * LANES
    total = devices * capacity
    return pl.pallas_call(
        functools.partial(pick_kernel, block),
        grid=(total // block,),
        in_specs=[
            pl.BlockSpec(memory_space=pltpu.SMEM),
            pl.BlockSpec(leaf2.shape, lambda s: (0, 0)),
        ],
        out_specs=pl.BlockSpec((2 * block, LANES), lambda s: (s, 0)),
        out_shape=jax.ShapeDtypeStruct((2 * total, LANES), jnp.bfloat16),
        scratch_shapes=[
            pltpu.VMEM(leaf2.shape, jnp.float32),
            pltpu.VMEM((2 * LANES, LANES), jnp.float32),
        ],
        compiler_params=pltpu.CompilerParams(vmem_limit_bytes=32 * 2**20),
        cost_estimate=pl.CostEstimate(flops=0, bytes_accessed=12 * 2**20, transcendentals=0),
    )(2 * chosen.reshape(total // LANES, LANES), leaf2)


def two_rows(x):
    return jnp.pad(x, ((0, 0), (0, 2 * LANES - x.shape[1]))).reshape(2 * x.shape[0], LANES)


def local(leaf_density, m2l_matrices, m2m_matrices, send_index, leaf_source, coarse_source):
    cells, width = leaf_density.shape
    noff = m2l_matrices.shape[0]
    parents_here = cells // 8
    devices, capacity = send_index.shape[1:]
    narrow = lax.axis_size("narrow")
    wide = lax.axis_size("wide")
    parents = jnp.dot(
        leaf_density.reshape(parents_here, 8 * width),
        m2m_matrices.reshape(8 * width, width),
        preferred_element_type=jnp.float32,
    ).astype(jnp.bfloat16)
    own = two_rows(parents)
    up = [(i, i + 1) for i in range(wide - 1)]
    down = [(j, i) for i, j in up]
    before = lax.ppermute(own, "wide", up)
    after = lax.ppermute(own, "wide", down)
    near = lax.all_gather(jnp.concatenate([before, own, after], axis=0), "narrow", axis=0, tiled=True)

    leaf2 = two_rows(leaf_density)
    outgoing = pick_rows(leaf2, send_index[0])
    far = lax.all_to_all(outgoing, ("wide", "narrow"), split_axis=0, concat_axis=0, tiled=True)

    group_rows = narrow * parents_here
    rel = coarse_source - (lax.axis_index("wide") - 1) * group_rows
    group, inside = rel // group_rows, rel % group_rows
    slot = (inside // parents_here) * (3 * parents_here) + group * parents_here + inside % parents_here
    coarse_row = jnp.where(coarse_source < 0, 0, 8 + 2 * (cells + devices * capacity + slot))
    leaf_row = jnp.where(leaf_source < 0, 0, 8 + 2 * leaf_source)
    used = cells + parents_here
    lines = -(-used // (8 * LANES)) * 8
    index = jnp.concatenate(
        [leaf_row, coarse_row, jnp.zeros((noff, lines * LANES - used), jnp.int32)], axis=1
    ).reshape(noff, lines, LANES)
    leaf_local, coarse_local = translate(index, m2l_matrices, leaf2, far, near, cells, parents_here)
    return (leaf_local, parents, coarse_local)


def solution(mesh):
    rows = P(("wide", "narrow"), None)
    columns = P(None, ("wide", "narrow"))
    return jax.shard_map(
        local,
        mesh=mesh,
        in_specs=(rows, P(), P(), P(("wide", "narrow"), None, None), columns, columns),
        out_specs=(rows, rows, rows),
        check_vma=False,
    )
```

time: 971 us -> 327 us (0.34)
  local copies, waits for them, and re-layouts: 754 us -> 31.2 us
  Pallas kernels: 0 us -> 164 us
  waiting for transfers between devices: 0.01 us -> 96.4 us
  other arithmetic: 93.5 us -> 1.97 us
  matrix products: 80.4 us -> 0.37 us
  blocking collectives: 14.8 us -> 0 us
  between operations: 0.86 us -> 14.2 us
    gather x28 -> x0, local copies, waits for them, and re-layouts: 554 us -> none  [step(): rows = jnp.take(table, pair[0], axis=0).reshape(targets, 27 * width)]
    pallas_call x0 -> x2, Pallas kernels: none -> 164 us  [the longest x1 147 us: translate(): pl.pallas_call(functools.partial(translate_kernel, leaves, tail), grid=(n...]
    select_n x28 -> x0, local copies, waits for them, and re-layouts: 128 us -> none  [step(): rows = jnp.take(table, pair[0], axis=0).reshape(targets, 27 * width)]
    select_n x30 -> x2, other arithmetic: 87.9 us -> 0.31 us  [the longest x1 0.23 us: local(): jnp.where(coarse_source < 0, 0, 8 + 2 * (cells + devices * capacity + slot))]
    dot_general x23 -> x1, matrix products: 80.4 us -> 0.37 us  [local(): jnp.dot(leaf_density.reshape(parents_here, 8 * width), m2m_matrices.resha...]
    ppermute x2, waiting for transfers between devices: 0.01 us -> 79.9 us  [the longest x1 79.9 us: local(): after = lax.ppermute(own, 'wide', down)]
    reshape x6 -> x4, local copies, waits for them, and re-layouts: 20.8 us -> 1.46 us  [the longest x1 0.94 us: local(): index = jnp.concatenate([leaf_row, coarse_row, jnp.zeros((noff, lines * L...]
    all_gather x0 -> x1, waiting for transfers between devices: none -> 16.5 us  [local(): lax.all_gather(jnp.concatenate([before, own, after], axis=0), 'narrow', a...]
  transfers between devices with their start and end apart: 3 -> 4, of which waited for: 0 -> 2; matrix products, arithmetic and copies ran while one was open for 20% -> 7% of each run, Pallas kernels for 0% -> 0%
where the time goes in v1:
time: 327 us; the launch traced here: 326 us
  Pallas kernels  164 us (50%)
  waiting for transfers between devices  96.4 us (29%)
  local copies, waits for them, and re-layouts  31.2 us (10%)
  starting transfers between devices  17.3 us (5%)
  between operations  14.2 us (4%)
    pallas_call x1, Pallas kernels, translate(): pl.pallas_call(functools.partial(translate_kernel, leaves, tail), grid=(n...  147 us
    ppermute x1, waiting for transfers between devices, local(): after = lax.ppermute(own, 'wide', down)  79.9 us
    unnamed x18, local copies, waits for them, and re-layouts  29.6 us
    pallas_call x1, Pallas kernels, pick_rows(): pl.pallas_call(functools.partial(pick_kernel, block), grid=(total // bloc...  17.3 us
    all_gather x1, waiting for transfers between devices, local(): lax.all_gather(jnp.concatenate([before, own, after], axis=0), 'narrow', a...  16.5 us
    all_to_all x1, starting transfers between devices, local(): lax.all_to_all(outgoing, ('wide', 'narrow'), split_axis=0, concat_axis=0,...  12 us
  transfers between devices with their start and end apart: 4, of which 2 were waited for; matrix products, arithmetic and copies ran while one was open for 7% of the time, Pallas kernels for 0%

profile of v1, /device:TPU:1, one launch (start us, length us, event | category | flops | bytes accessed | tf_op | source)
XLA Modules:
  0.0 325.7 jit_solution(10545253454318454426)
XLA Ops:
  7.2 0.0 copy-start
  7.2 0.9 multiply_bitcast_fusion.idx_ref
  8.1 1.1 copy.20
  9.2 0.1 pad.8.clone
  9.3 0.1 reshape.26.cells_ref.leaf_ref
  9.4 0.0 copy-start.2
  9.4 17.3 %shard_map.85 = bf16[32768,128]{1,0:T(8,128)(2,1)S(1)} custom-call(s32[128,128]{1,0:T(8,128)S(1)} %multiply_bitcast_fusion.idx_ref, bf16[1536,128]{1,0:T(8,128)(2,1)S(1)} %reshape.26.cells_ref.leaf_ref), custom_call_target="tpu_custom_call" | custom-call | bytes 12582912 | tf_op jit(solution)/shard_map/pallas_call | solution.py:146
  26.7 0.0 copy-start.1
  26.8 3.3 %copy-done.1 = bf16[32768,128]{1,0:T(8,128)(2,1)} copy-done((bf16[32768,128]{1,0:T(8,128)(2,1)}, bf16[32768,128]{1,0:T(8,128)(2,1)S(1)}, u32[]{:S(2)}) %copy-start.1) | copy-done | bytes 8388632
  30.1 0.0 copy-start.5
  30.1 0.0 copy-start.3
  30.1 0.0 copy-done.2
  30.1 12.0 %all-to-all-start = ((bf16[128,256,128]{2,1,0:T(8,128)(2,1)}), bf16[128,256,128]{2,1,0:T(8,128)(2,1)}, u32[]{:S(2)}, u32[]{:S(2)}) async-start(bf16[128,256,128]{2,1,0:T(8,128)(2,1)} %bitcast.11), calls=%async_computation | async-start | bytes 16777216 | tf_op jit(solution)/shard_map/all_to_all | solution.py:189
  42.0 0.0 all-gather.2.cloned.1.call-start
  42.1 0.4 reshape.27
  42.5 0.0 copy-done
  42.5 0.4 convolution_convert_fusion
  42.8 0.0 copy-start.4
  42.8 0.1 copy.21
  43.0 1.3 collective-permute-start.1
  44.3 4.0 %collective-permute-start = (bf16[192,128]{1,0:T(8,128)(2,1)S(1)}, bf16[192,128]{1,0:T(8,128)(2,1)S(1)}, u32[]{:S(2)}, u32[]{:S(2)}) collective-permute-start(bf16[192,128]{1,0:T(8,128)(2,1)S(1)} %reshape.29), channel_id=1, source_target_pairs={{0,8},{8,16},{16,24},{24,32},{32,40},{40,48},{48,56},{56,64},{64,7... | collective-permute-start | bytes 147464 | tf_op jit(solution)/shard_map/ppermute | solution.py:183
  48.3 79.9 %collective-permute-done.1 = bf16[192,128]{1,0:T(8,128)(2,1)S(1)} collective-permute-done((bf16[192,128]{1,0:T(8,128)(2,1)S(1)}, bf16[192,128]{1,0:T(8,128)(2,1)S(1)}, u32[]{:S(2)}, u32[]{:S(2)}) %collective-permute-start.1) | collective-permute-done | bytes 49184 | tf_op jit(solution)/shard_map/ppermute | solution.py:184
  128.2 0.0 collective-permute-done
  128.3 0.7 pad_maximum_fusion
  128.9 0.0 all-gather.2.cloned.1.call-update
  129.0 0.1 pad.15.clone
  129.0 0.0 copy-done.5
  129.0 0.2 fusion.6
  129.3 0.0 copy-done.3
  129.3 0.1 add_select_fusion
  129.4 0.1 add_add_fusion
  129.5 0.1 copy.22
  129.6 0.9 slice.idx_hbm
  130.6 21.1 %copy.17.m2l_ref = bf16[189,152,152]{2,1,0:T(8,128)(2,1)} copy(bf16[189,152,152]{0,2,1:T(8,128)(2,1)} %param.7) | data formatting | bytes 17466624 | tf_op args[1]
  151.7 0.0 copy-done.4
  151.7 16.5 %all-gather.2.cloned.1.call-done.near_ref = bf16[4608,128]{1,0:T(8,128)(2,1)} async-done(((bf16[576,128]{1,0:T(8,128)(2,1)}), bf16[4608,128]{1,0:T(8,128)(2,1)}) %all-gather.2.cloned.1.call-update) | async-done | bytes 1179664 | tf_op jit(solution)/shard_map/all_gather | solution.py:185
  168.2 0.0 all-to-all-done
  168.2 146.9 %shard_map.86 = (f32[768,152]{1,0:T(8,128)}, f32[96,152]{1,0:T(8,128)}) custom-call(s32[189,8,128]{2,1,0:T(8,128)} %slice.idx_hbm, bf16[189,152,152]{2,1,0:T(8,128)(2,1)} %copy.17.m2l_ref, bf16[1536,128]{1,0:T(8,128)(2,1)} %copy-done.2, bf16[32768,128]{1,0:T(8,128)(2,1)} %bitcast.2.far_ref, bf16[4608,128]{1,0:T(8,128)(2,1)} %all-gather.2.cloned.1.call-done.near_ref), custom_call_target="tpu_custom_call" | custom-call | flops 7545581568 | bytes 20971520 | tf_op jit(solution)/shard_map/pallas_call | solution.py:99
  315.1 2.1 copy.18
  317.2 1.6 copy.19
  (3 shorter events, 0.0 us)
Async XLA Ops:
  7.2 35.3 %copy-start = (bf16[8,152,152]{2,1,0:T(8,128)(2,1)S(1)}, bf16[8,152,152]{2,1,0:T(8,128)(2,1)}, u32[]{:S(2)}) copy-start(bf16[8,152,152]{2,1,0:T(8,128)(2,1)} %param.8) | copy-start | bytes 1108996
  9.4 20.7 %copy-start.2 = (bf16[1536,128]{1,0:T(8,128)(2,1)}, bf16[1536,128]{1,0:T(8,128)(2,1)S(1)}, u32[]{:S(2)}) copy-start(bf16[1536,128]{1,0:T(8,128)(2,1)S(1)} %reshape.26.cells_ref.leaf_ref) | copy-start | bytes 1179652
  26.7 3.3 %copy-start.1 = (bf16[32768,128]{1,0:T(8,128)(2,1)}, bf16[32768,128]{1,0:T(8,128)(2,1)S(1)}, u32[]{:S(2)}) copy-start(bf16[32768,128]{1,0:T(8,128)(2,1)S(1)} %shard_map.85) | copy-start | bytes 25165828
  30.1 99.0 %copy-start.5 = (s32[189,96]{1,0:T(8,128)S(1)}, s32[189,96]{1,0:T(8,128)}, u32[]{:S(2)}) copy-start(s32[189,96]{1,0:T(8,128)} %param.11) | copy-start | bytes 217732
  30.1 99.2 %copy-start.3 = (s32[189,768]{1,0:T(8,128)S(1)}, s32[189,768]{1,0:T(8,128)}, u32[]{:S(2)}) copy-start(s32[189,768]{1,0:T(8,128)} %param.10) | copy-start | bytes 1741828
  30.1 138.1 %all-to-all-start = ((bf16[128,256,128]{2,1,0:T(8,128)(2,1)}), bf16[128,256,128]{2,1,0:T(8,128)(2,1)}, u32[]{:S(2)}, u32[]{:S(2)}) async-start(bf16[128,256,128]{2,1,0:T(8,128)(2,1)} %bitcast.11), calls=%async_computation | async-start | bytes 16777216 | tf_op jit(solution)/shard_map/all_to_all | solution.py:189
  42.0 126.1 %all-gather.2.cloned.1.call-start = ((), (), s32[]{:S(2)}) async-start(), calls=%async_computation.1 | async-start | bytes 1327104 | tf_op jit(solution)/shard_map/all_gather | solution.py:185
  42.8 108.8 %copy-start.4 = (bf16[96,152]{0,1:T(8,128)(2,1)}, bf16[96,152]{0,1:T(8,128)(2,1)S(1)}, u32[]{:S(2)}) copy-start(bf16[96,152]{0,1:T(8,128)(2,1)S(1)} %convolution_convert_fusion) | copy-start | bytes 87556
  43.0 85.3 %collective-permute-start.1 = (bf16[192,128]{1,0:T(8,128)(2,1)S(1)}, bf16[192,128]{1,0:T(8,128)(2,1)S(1)}, u32[]{:S(2)}, u32[]{:S(2)}) collective-permute-start(bf16[192,128]{1,0:T(8,128)(2,1)S(1)} %reshape.29), channel_id=1, source_target_pairs={{8,0},{16,8},{24,16},{32,24},{40,32},{48,40},{56,48},{64,56},{72,6... | collective-permute-start | bytes 147464 | tf_op jit(solution)/shard_map/ppermute | solution.py:184
  44.3 84.0 %collective-permute-start = (bf16[192,128]{1,0:T(8,128)(2,1)S(1)}, bf16[192,128]{1,0:T(8,128)(2,1)S(1)}, u32[]{:S(2)}, u32[]{:S(2)}) collective-permute-start(bf16[192,128]{1,0:T(8,128)(2,1)S(1)} %reshape.29), channel_id=1, source_target_pairs={{0,8},{8,16},{16,24},{24,32},{32,40},{40,48},{48,56},{56,64},{64,7... | collective-permute-start | bytes 147464 | tf_op jit(solution)/shard_map/ppermute | solution.py:183
Sparse Core Ops, SparseCore 0:
  129.1 39.0 all-gather.1

commit v2 on v1

v2 whole, which is shorter than its diff:
```python
import functools

import jax
import jax.numpy as jnp
from jax import lax
from jax.experimental import pallas as pl
from jax.experimental.pallas import tpu as pltpu
from jax.sharding import PartitionSpec as P

LANES = 128
SPLIT = 4
RING = 3
ZERO = 8
PARTS = 8


def place_far(block, table, base):
    count = block.shape[0] - LANES // SPLIT
    rows, step = count // SPLIT, LANES // SPLIT
    table[pl.ds(base, count, stride=2), :] = block[0:count].astype(jnp.float32)
    rest = block[count:].astype(jnp.float32)
    for j in range(SPLIT):
        part = rest if j == 0 else pltpu.roll(rest, LANES - j * step, axis=1)
        table[pl.ds(base + 1 + 2 * j * rows, rows, stride=2), :] = part


def translate_kernel(group, count, scale, packed, halves, idx_hbm, m2l_ref, *refs):
    near_ref, refs = refs[0], refs[1:]
    if packed:
        far_hbm, refs = refs[0], refs[1:]
    out_ref, table, acc, idx_vmem = refs[:4]
    rows_f, mats, smem = refs[4:7], refs[7:10], refs[10:13]
    sem, vsem = refs[13:15]
    step = pl.program_id(0)
    steps = pl.num_programs(0)
    width = m2l_ref.shape[1]
    total = group * count

    def fetch(k, s):
        return pltpu.make_async_copy(idx_vmem.at[RING * s + k], smem[k], sem.at[k])

    def gather(k, lo, hi):
        for t in range(lo, hi):
            i = smem[k][t // LANES, t % LANES]
            rows_f[k][pl.ds(2 * t, 2), :] = table[pl.ds(i, 2), :]

    def multiply(k, lo, hi):
        n = min(hi - lo, count)
        at = lo % count if group > 1 else lo
        result = acc[at:at + n]
        for g in range(lo // count, -(-hi // count)):
            first = 2 * max(lo, g * count)
            low = rows_f[k][pl.ds(first, n, stride=2), :].astype(jnp.bfloat16)
            high = rows_f[k][pl.ds(first + 1, n, stride=2), :].astype(jnp.bfloat16)
            result += jnp.dot(jnp.concatenate([low, high], axis=1), mats[k][g], preferred_element_type=jnp.float32)
        acc[at:at + n] = result

    def load_matrix(k):
        for g in range(group):
            mats[k][g, 0:width, 0:width] = m2l_ref[k * group + g]

    @pl.when(step == 0)
    def _():
        copy = pltpu.make_async_copy(idx_hbm, idx_vmem, vsem)
        copy.start()
        if packed:
            far, fsem = refs[15:17]
            span = far.shape[0] // PARTS

            def part(q):
                return pltpu.make_async_copy(far_hbm.at[pl.ds(q * span, span)], far.at[pl.ds(q * span, span)], fsem.at[q])

            for q in range(PARTS):
                part(q).start()
        acc[...] = jnp.zeros_like(acc)
        rows_f[RING - 1][...] = jnp.zeros_like(rows_f[RING - 1])
        for w in mats:
            w[...] = jnp.zeros_like(w)
        table[0:ZERO, :] = jnp.zeros((ZERO, LANES), jnp.float32)
        n = near_ref.shape[0]
        table[pl.ds(ZERO, n), :] = near_ref[...].astype(jnp.float32)
        if packed:
            for q in range(PARTS):
                part(q).wait()

                @pl.loop(0, span)
                def _(b):
                    p = q * span + b
                    place_far(far[p], table, pl.multiple_of(ZERO + n + p * 2 * (far.shape[1] - LANES // SPLIT), 8))
        copy.wait()
        for k in range(RING):
            fetch(k, 0).start()

    for k in range(RING):
        fetch(k, step).wait()
        if k == 1:
            for j in range(RING):
                load_matrix(j)
        for lo, hi in zip(halves, halves[1:]):
            gather(k, lo, hi)
            multiply((k + RING - 1) % RING, lo, hi)

        @pl.when(step + 1 < steps)
        def _():
            fetch(k, step + 1).start()

    @pl.when(step == steps - 1)
    def _():
        for lo, hi in zip(halves, halves[1:]):
            multiply(RING - 1, lo, hi)
        out_ref[...] = scale * acc[:, 0:width] if scale != 1 else acc[:, 0:width]


def translate(idx, m2l, near2, far, group, count, scale, halves):
    noff, width, _ = m2l.shape
    rows = ZERO + near2.shape[0]
    total = group * count
    operands = [idx, m2l, near2]
    in_specs = [
        pl.BlockSpec(memory_space=pl.ANY),
        pl.BlockSpec((RING * group, width, width), lambda s: (s, 0, 0)),
        pl.BlockSpec(near2.shape, lambda s: (0, 0), pipeline_mode=pl.Buffered(1)),
    ]
    extra = []
    if far is not None:
        rows += 2 * far.shape[0] * (far.shape[1] - LANES // SPLIT)
        operands.append(far)
        in_specs.append(pl.BlockSpec(memory_space=pl.ANY))
        extra = [pltpu.VMEM(far.shape, far.dtype), pltpu.SemaphoreType.DMA((PARTS,))]
    return pl.pallas_call(
        functools.partial(translate_kernel, group, count, scale, far is not None, halves),
        grid=(noff // (RING * group),),
        in_specs=in_specs,
        out_specs=pl.BlockSpec((count, width), lambda s: (0, 0)),
        out_shape=jax.ShapeDtypeStruct((count, width), jnp.float32),
        scratch_shapes=[
            pltpu.VMEM((rows, LANES), jnp.float32),
            pltpu.VMEM((count, 2 * LANES), jnp.float32),
            pltpu.VMEM(idx.shape, jnp.int32),
        ] + [pltpu.VMEM((2 * total, LANES), jnp.float32)] * RING
        + [pltpu.VMEM((group, 2 * LANES, 2 * LANES), jnp.bfloat16)] * RING
        + [pltpu.SMEM(idx.shape[1:], jnp.int32)] * RING
        + [pltpu.SemaphoreType.DMA((RING,)), pltpu.SemaphoreType.DMA] + extra,
        compiler_params=pltpu.CompilerParams(vmem_limit_bytes=(50 if far is not None else 32) * 2**20),
        cost_estimate=pl.CostEstimate(
            flops=2 * noff * count * 256 * 256 * 3, bytes_accessed=20 * 2**20, transcendentals=0),
    )(*operands)


def pick_kernel(capacity, idx_hbm, cells_ref, out_ref, table, f0, f1, s0, s1, sem):
    step = pl.program_id(0)
    steps = pl.num_programs(0)
    rows_f, smem = (f0, f1), (s0, s1)
    lines = s0.shape[0]
    rows, lane = capacity // SPLIT, LANES // SPLIT

    def fetch(k, s):
        return pltpu.make_async_copy(idx_hbm.at[pl.ds((2 * s + k) * lines, lines)], smem[k], sem.at[k])

    @pl.when(step == 0)
    def _():
        for k in range(2):
            fetch(k, 0).start()
        table[...] = cells_ref[...].astype(jnp.float32)

    for k in range(2):
        fetch(k, step).wait()
        for r in range(lines):
            for u in range(capacity):
                rows_f[k][pl.ds(2 * (r * capacity + u), 2), :] = table[pl.ds(smem[k][r, u], 2), :]
            base = 2 * r * capacity
            out_ref[k * lines + r, 0:capacity] = rows_f[k][pl.ds(base, capacity, stride=2), :].astype(jnp.bfloat16)
            rest = rows_f[k][pl.ds(base + 1, rows, stride=2), :]
            for j in range(1, SPLIT):
                part = rows_f[k][pl.ds(base + 1 + 2 * j * rows, rows, stride=2), :]
                rest += pltpu.roll(part, j * lane, axis=1)
            out_ref[k * lines + r, capacity:] = rest.astype(jnp.bfloat16)

        @pl.when(step + 1 < steps)
        def _():
            fetch(k, step + 1).start()


def pick_rows(leaf2, chosen):
    devices, capacity = chosen.shape
    lines = 8
    return pl.pallas_call(
        functools.partial(pick_kernel, capacity),
        grid=(devices // (2 * lines),),
        in_specs=[
            pl.BlockSpec(memory_space=pl.ANY),
            pl.BlockSpec(leaf2.shape, lambda s: (0, 0)),
        ],
        out_specs=pl.BlockSpec((2 * lines, capacity + capacity // SPLIT, LANES), lambda s: (s, 0, 0)),
        out_shape=jax.ShapeDtypeStruct((devices, capacity + capacity // SPLIT, LANES), jnp.bfloat16),
        scratch_shapes=[pltpu.VMEM(leaf2.shape, jnp.float32)]
        + [pltpu.VMEM((2 * lines * capacity, LANES), jnp.float32)] * 2
        + [pltpu.SMEM((lines, capacity), jnp.int32)] * 2
        + [pltpu.SemaphoreType.DMA((2,))],
        compiler_params=pltpu.CompilerParams(vmem_limit_bytes=32 * 2**20),
        cost_estimate=pl.CostEstimate(flops=0, bytes_accessed=32 * 2**20, transcendentals=0),
    )(2 * chosen, leaf2)


def two_rows(x):
    return jnp.pad(x, ((0, 0), (0, 2 * LANES - x.shape[1]))).reshape(2 * x.shape[0], LANES)


def lines_of(index):
    used = index.shape[1]
    lines = -(-used // LANES)
    return jnp.pad(index, ((0, 0), (0, lines * LANES - used))).reshape(index.shape[0], lines, LANES)


def local(leaf_density, m2l_matrices, m2m_matrices, send_index, leaf_source, coarse_source):
    cells, width = leaf_density.shape
    noff = m2l_matrices.shape[0]
    parents_here = cells // 8
    narrow = lax.axis_size("narrow")
    wide = lax.axis_size("wide")
    parents = jnp.dot(
        leaf_density.reshape(parents_here, 8 * width),
        m2m_matrices.reshape(8 * width, width),
        preferred_element_type=jnp.float32,
    ).astype(jnp.bfloat16)
    own = two_rows(parents)
    up = [(i, i + 1) for i in range(wide - 1)]
    down = [(j, i) for i, j in up]
    before = lax.ppermute(own, "wide", up)
    after = lax.ppermute(own, "wide", down)
    near = lax.all_gather(jnp.concatenate([before, own, after], axis=0), "narrow", axis=0, tiled=True)

    leaf2 = two_rows(leaf_density)
    outgoing = pick_rows(leaf2, send_index[0])
    outgoing, near, m2l_matrices, leaf_source, coarse_source = lax.optimization_barrier(
        (outgoing, near, m2l_matrices, leaf_source, coarse_source)
    )
    far = lax.all_to_all(outgoing, ("wide", "narrow"), split_axis=0, concat_axis=0, tiled=True)

    group_rows = narrow * parents_here
    rel = coarse_source - (lax.axis_index("wide") - 1) * group_rows
    group, inside = rel // group_rows, rel % group_rows
    slot = (inside // parents_here) * (3 * parents_here) + group * parents_here + inside % parents_here
    coarse_row = jnp.where(coarse_source < 0, 0, ZERO + 2 * slot)
    together = 9
    coarse_index = lines_of(coarse_row.reshape(noff // together, together * parents_here))
    bounds = tuple(together * parents_here * h // 3 for h in range(4))
    coarse_local = translate(coarse_index, m2l_matrices, near, None, together, parents_here, 0.5, bounds)

    leaf_index = lines_of(jnp.where(leaf_source < 0, 0, ZERO + 2 * leaf_source))
    far, leaf_index, coarse_local = lax.optimization_barrier((far, leaf_index, coarse_local))
    leaf_local = translate(leaf_index, m2l_matrices, leaf2, far, 1, cells, 1, (0, cells // 2, cells))
    return (leaf_local, parents, coarse_local)


def solution(mesh):
    rows = P(("wide", "narrow"), None)
    columns = P(None, ("wide", "narrow"))
    return jax.shard_map(
        local,
        mesh=mesh,
        in_specs=(rows, P(), P(), P(("wide", "narrow"), None, None), columns, columns),
        out_specs=(rows, rows, rows),
        check_vma=False,
    )
```

time: 327 us -> 250 us (0.76)
  waiting for transfers between devices: 96.4 us -> 32.6 us
  Pallas kernels: 164 us -> 152 us
    ppermute x1, waiting for transfers between devices: 79.9 us -> 0.01 us  [local(): after = lax.ppermute(own, 'wide', down)]
    optimization_barrier x0 -> x1, local copies, waits for them, and re-layouts: none -> 21.1 us  [local(): lax.optimization_barrier((outgoing, near, m2l_matrices, leaf_source, coar...]
    all_to_all x1, waiting for transfers between devices: 0.01 us -> 18.4 us  [local(): lax.all_to_all(outgoing, ('wide', 'narrow'), split_axis=0, concat_axis=0,...]
    unnamed x18, local copies, waits for them, and re-layouts: 29.6 us -> 11.7 us
    pallas_call x2 -> x3, Pallas kernels: 164 us -> 152 us  [the longest x2 138 us: translate(): pl.pallas_call(functools.partial(translate_kernel, group, count, scale, f...]
    all_to_all x1, starting transfers between devices: 12 us -> 8.32 us  [local(): lax.all_to_all(outgoing, ('wide', 'narrow'), split_axis=0, concat_axis=0,...]
    all_gather x1, waiting for transfers between devices: 16.5 us -> 13 us  [local(): lax.all_gather(jnp.concatenate([before, own, after], axis=0), 'narrow', a...]
  transfers between devices with their start and end apart: 4 -> 4, of which waited for: 2 -> 3; matrix products, arithmetic and copies ran while one was open for 7% -> 9% of each run, Pallas kernels for 0% -> 13%
where the time goes in v2:
time: 250 us; the launch traced here: 249 us
  Pallas kernels  152 us (61%)
  local copies, waits for them, and re-layouts  33.7 us (13%)
  waiting for transfers between devices  32.6 us (13%)
  starting transfers between devices  14.7 us (6%)
  between operations  14.2 us (6%)
    pallas_call x2, Pallas kernels, translate(): pl.pallas_call(functools.partial(translate_kernel, group, count, scale, f...  138 us
    optimization_barrier x1, local copies, waits for them, and re-layouts, local(): lax.optimization_barrier((outgoing, near, m2l_matrices, leaf_source, coar...  21.1 us
    all_to_all x1, waiting for transfers between devices, local(): lax.all_to_all(outgoing, ('wide', 'narrow'), split_axis=0, concat_axis=0,...  18.4 us
    pallas_call x1, Pallas kernels, pick_rows(): pl.pallas_call(functools.partial(pick_kernel, capacity), grid=(devices //...  14.2 us
    all_gather x1, waiting for transfers between devices, local(): lax.all_gather(jnp.concatenate([before, own, after], axis=0), 'narrow', a...  13 us
    unnamed x18, local copies, waits for them, and re-layouts  11.7 us
    all_to_all x1, starting transfers between devices, local(): lax.all_to_all(outgoing, ('wide', 'narrow'), split_axis=0, concat_axis=0,...  8.32 us
    ppermute x1, starting transfers between devices, local(): before = lax.ppermute(own, 'wide', up)  5 us
  transfers between devices with their start and end apart: 4, of which 3 were waited for; matrix products, arithmetic and copies ran while one was open for 9% of the time, Pallas kernels for 13%

profile of v2, /device:TPU:1, one launch (start us, length us, event | category | flops | bytes accessed | tf_op | source)
XLA Modules:
  0.0 249.3 jit_solution(7265771481975253893)
XLA Ops:
  7.2 0.0 copy-start
  7.2 0.0 all-gather.2.cloned.1.call-start
  7.2 1.2 copy.22
  8.4 0.4 reshape.30
  8.8 0.0 copy-done
  8.8 0.4 convolution_convert_fusion
  9.1 0.0 copy-start.5
  9.2 0.1 copy.23
  9.3 1.3 collective-permute-start.1
  10.6 5.0 %collective-permute-start = (bf16[192,128]{1,0:T(8,128)(2,1)S(1)}, bf16[192,128]{1,0:T(8,128)(2,1)S(1)}, u32[]{:S(2)}, u32[]{:S(2)}) collective-permute-start(bf16[192,128]{1,0:T(8,128)(2,1)S(1)} %reshape.32), channel_id=1, source_target_pairs={{0,8},{8,16},{16,24},{24,32},{32,40},{40,48},{48,56},{56,64},{64,7... | collective-permute-start | bytes 147464 | tf_op jit(solution)/shard_map/ppermute | solution.py:229
  15.6 0.0 collective-permute-done.1
  15.6 1.1 collective-permute-done
  16.8 0.7 pad_maximum_fusion
  17.4 0.0 all-gather.2.cloned.1.call-update
  17.5 0.1 pad.12.clone
  17.5 0.1 reshape.29.cells_ref.refs_0_
  17.7 0.8 multiply_bitcast_fusion.idx_hbm
  18.5 14.2 %shard_map.85 = bf16[128,160,128]{2,1,0:T(8,128)(2,1)S(1)} custom-call(s32[128,128]{1,0:T(8,128)S(1)} %multiply_bitcast_fusion.idx_hbm, bf16[1536,128]{1,0:T(8,128)(2,1)S(1)} %reshape.29.cells_ref.refs_0_), custom_call_target="tpu_custom_call" | custom-call | bytes 33554432 | tf_op jit(solution)/shard_map/pallas_call | solution.py:187
  32.7 0.0 copy-start.1
  32.7 2.3 copy-done.1
  35.0 0.0 copy-start.6
  35.0 0.0 copy-start.4
  35.0 13.0 %all-gather.2.cloned.1.call-done.refs_0_ = bf16[4608,128]{1,0:T(8,128)(2,1)} async-done(((bf16[576,128]{1,0:T(8,128)(2,1)}), bf16[4608,128]{1,0:T(8,128)(2,1)}) %all-gather.2.cloned.1.call-update) | async-done | bytes 1179664 | tf_op jit(solution)/shard_map/all_gather | solution.py:231
  48.0 0.0 copy-done.5
  48.0 8.3 %all-to-all-start = ((bf16[128,160,128]{2,1,0:T(8,128)(2,1)}), bf16[128,160,128]{2,1,0:T(8,128)(2,1)}, u32[]{:S(2)}, u32[]{:S(2)}) async-start(bf16[128,160,128]{2,1,0:T(8,128)(2,1)} %copy-done.1), calls=%async_computation | async-start | bytes 10485760 | tf_op jit(solution)/shard_map/all_to_all | solution.py:238
  56.3 0.0 copy-done.6
  56.4 0.2 fusion.5
  56.6 0.1 reshape.34
  56.7 0.0 copy-done.4
  56.7 0.1 add_select_fusion
  56.8 0.1 reshape.33.idx_hbm
  56.9 21.1 %copy.18.m2l_ref = bf16[189,152,152]{2,1,0:T(8,128)(2,1)} copy(bf16[189,152,152]{0,2,1:T(8,128)(2,1)} %param.7) | data formatting | bytes 17466624 | tf_op jit(solution)/shard_map/optimization_barrier | solution.py:235
  78.0 0.0 copy-start.2
  78.0 5.2 %copy-done.2 = bf16[189,152,152]{2,1,0:T(8,128)(2,1)S(1)} copy-done((bf16[189,152,152]{2,1,0:T(8,128)(2,1)S(1)}, bf16[189,152,152]{2,1,0:T(8,128)(2,1)}, u32[]{:S(2)}) %copy-start.2) | copy-done | bytes 8733336
  83.2 0.0 copy-start.3
  83.2 1.3 copy-done.3
  84.5 18.0 %shard_map.86 = f32[96,152]{1,0:T(8,128)S(1)} custom-call(s32[21,7,128]{2,1,0:T(8,128)S(1)} %reshape.35.idx_hbm, bf16[189,152,152]{2,1,0:T(8,128)(2,1)S(1)} %copy-done.2, bf16[4608,128]{1,0:T(8,128)(2,1)S(1)} %copy-done.3), custom_call_target="tpu_custom_call" | custom-call | flops 7134511104 | bytes 20971520 | tf_op jit(solution)/shard_map/pallas_call | solution.py:130
  102.5 18.4 %all-to-all-done.refs_1_ = bf16[128,160,128]{2,1,0:T(8,128)(2,1)} async-done(((bf16[128,160,128]{2,1,0:T(8,128)(2,1)}), bf16[128,160,128]{2,1,0:T(8,128)(2,1)}, u32[]{:S(2)}, u32[]{:S(2)}) %all-to-all-start) | async-done | bytes 5242912 | tf_op jit(solution)/shard_map/all_to_all | solution.py:238
  120.9 119.8 %shard_map.87 = f32[768,152]{1,0:T(8,128)S(1)} custom-call(s32[189,6,128]{2,1,0:T(8,128)S(1)} %reshape.33.idx_hbm, bf16[189,152,152]{2,1,0:T(8,128)(2,1)} %copy.18.m2l_ref, bf16[1536,128]{1,0:T(8,128)(2,1)S(1)} %reshape.29.cells_ref.refs_0_, bf16[128,160,128]{2,1,0:T(8,128)(2,1)} %all-to-all-done.refs_1_), custom_call_target="tpu_custom_call" | custom-call | flops 57076088832 | bytes 20971520 | tf_op jit(solution)/shard_map/pallas_call | solution.py:130
  240.7 1.0 copy.20
  241.7 0.7 copy.21
  (4 shorter events, 0.1 us)
Async XLA Ops:
  7.2 1.6 copy-start
  7.2 40.8 %all-gather.2.cloned.1.call-start = ((), (), s32[]{:S(2)}) async-start(), calls=%async_computation.1 | async-start | bytes 1327104 | tf_op jit(solution)/shard_map/all_gather | solution.py:231
  9.1 38.9 %copy-start.5 = (bf16[96,152]{0,1:T(8,128)(2,1)}, bf16[96,152]{0,1:T(8,128)(2,1)S(1)}, u32[]{:S(2)}) copy-start(bf16[96,152]{0,1:T(8,128)(2,1)S(1)} %convolution_convert_fusion) | copy-start | bytes 87556
  9.3 6.3 %collective-permute-start.1 = (bf16[192,128]{1,0:T(8,128)(2,1)S(1)}, bf16[192,128]{1,0:T(8,128)(2,1)S(1)}, u32[]{:S(2)}, u32[]{:S(2)}) collective-permute-start(bf16[192,128]{1,0:T(8,128)(2,1)S(1)} %reshape.32), channel_id=1, source_target_pairs={{8,0},{16,8},{24,16},{32,24},{40,32},{48,40},{56,48},{64,56},{72,6... | collective-permute-start | bytes 147464 | tf_op jit(solution)/shard_map/ppermute | solution.py:230
  10.6 6.2 %collective-permute-start = (bf16[192,128]{1,0:T(8,128)(2,1)S(1)}, bf16[192,128]{1,0:T(8,128)(2,1)S(1)}, u32[]{:S(2)}, u32[]{:S(2)}) collective-permute-start(bf16[192,128]{1,0:T(8,128)(2,1)S(1)} %reshape.32), channel_id=1, source_target_pairs={{0,8},{8,16},{16,24},{24,32},{32,40},{40,48},{48,56},{56,64},{64,7... | collective-permute-start | bytes 147464 | tf_op jit(solution)/shard_map/ppermute | solution.py:229
  32.7 2.3 copy-start.1
  35.0 21.4 %copy-start.6 = (s32[189,96]{1,0:T(8,128)S(1)}, s32[189,96]{1,0:T(8,128)}, u32[]{:S(2)}) copy-start(s32[189,96]{1,0:T(8,128)} %param.11) | copy-start | bytes 217732
  35.0 21.8 %copy-start.4 = (s32[189,768]{1,0:T(8,128)S(1)}, s32[189,768]{1,0:T(8,128)}, u32[]{:S(2)}) copy-start(s32[189,768]{1,0:T(8,128)} %param.10) | copy-start | bytes 1741828
  48.0 72.9 %all-to-all-start = ((bf16[128,160,128]{2,1,0:T(8,128)(2,1)}), bf16[128,160,128]{2,1,0:T(8,128)(2,1)}, u32[]{:S(2)}, u32[]{:S(2)}) async-start(bf16[128,160,128]{2,1,0:T(8,128)(2,1)} %copy-done.1), calls=%async_computation | async-start | bytes 10485760 | tf_op jit(solution)/shard_map/all_to_all | solution.py:238
  78.0 5.2 %copy-start.2 = (bf16[189,152,152]{2,1,0:T(8,128)(2,1)S(1)}, bf16[189,152,152]{2,1,0:T(8,128)(2,1)}, u32[]{:S(2)}) copy-start(bf16[189,152,152]{2,1,0:T(8,128)(2,1)} %copy.18.m2l_ref) | copy-start | bytes 26199940
  83.2 1.3 copy-start.3
Sparse Core Ops, SparseCore 0:
  17.6 30.3 all-gather.1

commit v3 on v2

--- a/solution.py
+++ b/solution.py
@@ -12,6 +12,9 @@
 RING = 3
 ZERO = 8
 PARTS = 8
+LEAF_GROUP = 1
+LEAF_BURST = 9
+LEAF_PIECES = 2
 
 
 def place_far(block, table, base):
@@ -24,7 +27,7 @@
         table[pl.ds(base + 1 + 2 * j * rows, rows, stride=2), :] = part
 
 
-def translate_kernel(group, count, scale, packed, halves, idx_hbm, m2l_ref, *refs):
+def translate_kernel(group, count, scale, packed, burst, pieces, idx_hbm, m2l_ref, *refs):
     near_ref, refs = refs[0], refs[1:]
     if packed:
         far_hbm, refs = refs[0], refs[1:]
@@ -36,8 +39,8 @@
     width = m2l_ref.shape[1]
     total = group * count
 
-    def fetch(k, s):
-        return pltpu.make_async_copy(idx_vmem.at[RING * s + k], smem[k], sem.at[k])
+    def fetch(k, c):
+        return pltpu.make_async_copy(idx_vmem.at[c], smem[k], sem.at[k])
 
     def gather(k, lo, hi):
         for t in range(lo, hi):
@@ -45,19 +48,16 @@
             rows_f[k][pl.ds(2 * t, 2), :] = table[pl.ds(i, 2), :]
 
     def multiply(k, lo, hi):
-        n = min(hi - lo, count)
-        at = lo % count if group > 1 else lo
-        result = acc[at:at + n]
-        for g in range(lo // count, -(-hi // count)):
-            first = 2 * max(lo, g * count)
-            low = rows_f[k][pl.ds(first, n, stride=2), :].astype(jnp.bfloat16)
-            high = rows_f[k][pl.ds(first + 1, n, stride=2), :].astype(jnp.bfloat16)
-            result += jnp.dot(jnp.concatenate([low, high], axis=1), mats[k][g], preferred_element_type=jnp.float32)
-        acc[at:at + n] = result
-
-    def load_matrix(k):
+        sides = []
         for g in range(group):
-            mats[k][g, 0:width, 0:width] = m2l_ref[k * group + g]
+            for side in range(2):
+                rows = pl.ds(2 * (g * count + lo) + side, hi - lo, stride=2)
+                sides.append(rows_f[k][rows, :].astype(jnp.bfloat16))
+        acc[lo:hi] += jnp.dot(jnp.concatenate(sides, axis=1), mats[k][...], preferred_element_type=jnp.float32)
+
+    def load_matrix(k, c):
+        for g in range(group):
+            mats[k][2 * LANES * g:2 * LANES * g + width, 0:width] = m2l_ref[c * group + g]
 
     @pl.when(step == 0)
     def _():
@@ -73,7 +73,8 @@
             for q in range(PARTS):
                 part(q).start()
         acc[...] = jnp.zeros_like(acc)
-        rows_f[RING - 1][...] = jnp.zeros_like(rows_f[RING - 1])
+        last = rows_f[(burst - 1) % RING]
+        last[...] = jnp.zeros_like(last)
         for w in mats:
             w[...] = jnp.zeros_like(w)
         table[0:ZERO, :] = jnp.zeros((ZERO, LANES), jnp.float32)
@@ -89,36 +90,34 @@
                     place_far(far[p], table, pl.multiple_of(ZERO + n + p * 2 * (far.shape[1] - LANES // SPLIT), 8))
         copy.wait()
         for k in range(RING):
-            fetch(k, 0).start()
-
-    for k in range(RING):
-        fetch(k, step).wait()
-        if k == 1:
-            for j in range(RING):
-                load_matrix(j)
-        for lo, hi in zip(halves, halves[1:]):
-            gather(k, lo, hi)
-            multiply((k + RING - 1) % RING, lo, hi)
-
-        @pl.when(step + 1 < steps)
+            fetch(k, k).start()
+
+    for c in range(burst):
+        k = c % RING
+        fetch(k, burst * step + c).wait()
+        load_matrix(k, c)
+        for p in range(pieces):
+            gather(k, total * p // pieces, total * (p + 1) // pieces)
+            multiply((c + burst - 1) % burst % RING, count * p // pieces, count * (p + 1) // pieces)
+
+        @pl.when(burst * step + c + RING < burst * steps)
         def _():
-            fetch(k, step + 1).start()
+            fetch(k, burst * step + c + RING).start()
 
     @pl.when(step == steps - 1)
     def _():
-        for lo, hi in zip(halves, halves[1:]):
-            multiply(RING - 1, lo, hi)
+        multiply((burst - 1) % RING, 0, count)
         out_ref[...] = scale * acc[:, 0:width] if scale != 1 else acc[:, 0:width]
 
 
-def translate(idx, m2l, near2, far, group, count, scale, halves):
+def translate(idx, m2l, near2, far, group, count, scale, burst, pieces):
     noff, width, _ = m2l.shape
     rows = ZERO + near2.shape[0]
     total = group * count
     operands = [idx, m2l, near2]
     in_specs = [
         pl.BlockSpec(memory_space=pl.ANY),
-        pl.BlockSpec((RING * group, width, width), lambda s: (s, 0, 0)),
+        pl.BlockSpec((burst * group, width, width), lambda s: (s, 0, 0)),
         pl.BlockSpec(near2.shape, lambda s: (0, 0), pipeline_mode=pl.Buffered(1)),
     ]
     extra = []
@@ -128,8 +127,8 @@
         in_specs.append(pl.BlockSpec(memory_space=pl.ANY))
         extra = [pltpu.VMEM(far.shape, far.dtype), pltpu.SemaphoreType.DMA((PARTS,))]
     return pl.pallas_call(
-        functools.partial(translate_kernel, group, count, scale, far is not None, halves),
-        grid=(noff // (RING * group),),
+        functools.partial(translate_kernel, group, count, scale, far is not None, burst, pieces),
+        grid=(noff // (burst * group),),
         in_specs=in_specs,
         out_specs=pl.BlockSpec((count, width), lambda s: (0, 0)),
         out_shape=jax.ShapeDtypeStruct((count, width), jnp.float32),
@@ -138,10 +137,10 @@
             pltpu.VMEM((count, 2 * LANES), jnp.float32),
             pltpu.VMEM(idx.shape, jnp.int32),
         ] + [pltpu.VMEM((2 * total, LANES), jnp.float32)] * RING
-        + [pltpu.VMEM((group, 2 * LANES, 2 * LANES), jnp.bfloat16)] * RING
+        + [pltpu.VMEM((group * 2 * LANES, 2 * LANES), jnp.bfloat16)] * RING
         + [pltpu.SMEM(idx.shape[1:], jnp.int32)] * RING
         + [pltpu.SemaphoreType.DMA((RING,)), pltpu.SemaphoreType.DMA] + extra,
-        compiler_params=pltpu.CompilerParams(vmem_limit_bytes=(50 if far is not None else 32) * 2**20),
+        compiler_params=pltpu.CompilerParams(vmem_limit_bytes=56 * 2**20),
         cost_estimate=pl.CostEstimate(
             flops=2 * noff * count * 256 * 256 * 3, bytes_accessed=20 * 2**20, transcendentals=0),
     )(*operands)
@@ -197,7 +196,7 @@
         + [pltpu.VMEM((2 * lines * capacity, LANES), jnp.float32)] * 2
         + [pltpu.SMEM((lines, capacity), jnp.int32)] * 2
         + [pltpu.SemaphoreType.DMA((2,))],
-        compiler_params=pltpu.CompilerParams(vmem_limit_bytes=32 * 2**20),
+        compiler_params=pltpu.CompilerParams(vmem_limit_bytes=56 * 2**20),
         cost_estimate=pl.CostEstimate(flops=0, bytes_accessed=32 * 2**20, transcendentals=0),
     )(2 * chosen, leaf2)
 
@@ -228,7 +227,10 @@
     down = [(j, i) for i, j in up]
     before = lax.ppermute(own, "wide", up)
     after = lax.ppermute(own, "wide", down)
-    near = lax.all_gather(jnp.concatenate([before, own, after], axis=0), "narrow", axis=0, tiled=True)
+    three = jnp.concatenate([before, own, after], axis=0)
+    near = lax.all_to_all(
+        jnp.broadcast_to(three, (narrow,) + three.shape), "narrow", split_axis=0, concat_axis=0, tiled=True
+    ).reshape(narrow * three.shape[0], LANES)
 
     leaf2 = two_rows(leaf_density)
     outgoing = pick_rows(leaf2, send_index[0])
@@ -244,12 +246,13 @@
     coarse_row = jnp.where(coarse_source < 0, 0, ZERO + 2 * slot)
     together = 9
     coarse_index = lines_of(coarse_row.reshape(noff // together, together * parents_here))
-    bounds = tuple(together * parents_here * h // 3 for h in range(4))
-    coarse_local = translate(coarse_index, m2l_matrices, near, None, together, parents_here, 0.5, bounds)
-
-    leaf_index = lines_of(jnp.where(leaf_source < 0, 0, ZERO + 2 * leaf_source))
+    coarse_local = translate(coarse_index, m2l_matrices, near, None, together, parents_here, 0.5, 3, 1)
+
+    leaf_index = lines_of(
+        jnp.where(leaf_source < 0, 0, ZERO + 2 * leaf_source).reshape(noff // LEAF_GROUP, LEAF_GROUP * cells)
+    )
     far, leaf_index, coarse_local = lax.optimization_barrier((far, leaf_index, coarse_local))
-    leaf_local = translate(leaf_index, m2l_matrices, leaf2, far, 1, cells, 1, (0, cells // 2, cells))
+    leaf_local = translate(leaf_index, m2l_matrices, leaf2, far, LEAF_GROUP, cells, 1, LEAF_BURST, LEAF_PIECES)
     return (leaf_local, parents, coarse_local)
 
 

time: 250 us -> 234 us (0.936)
  between operations: 14.2 us -> 0.85 us
  starting transfers between devices: 14.7 us -> 26.1 us
  waiting for transfers between devices: 32.6 us -> 21.4 us
  local copies, waits for them, and re-layouts: 33.7 us -> 30.6 us
    all_gather x1 -> x0, waiting for transfers between devices: 13 us -> none  [local(): lax.all_gather(jnp.concatenate([before, own, after], axis=0), 'narrow', a...]
    unnamed x18, local copies, waits for them, and re-layouts: 11.7 us -> 5.26 us
    all_to_all x0 -> x1, starting transfers between devices: none -> 6.09 us  [local(): lax.all_to_all(jnp.broadcast_to(three, (narrow,) + three.shape), 'narrow'...]
    all_to_all x1, starting transfers between devices: 8.32 us -> 13.7 us  [local(): lax.all_to_all(outgoing, ('wide', 'narrow'), split_axis=0, concat_axis=0,...]
  transfers between devices with their start and end apart: 4 -> 4, of which waited for: 3 -> 2; matrix products, arithmetic and copies ran while one was open for 9% -> 11% of each run, Pallas kernels for 13% -> 16%
where the time goes in v3:
time: 234 us; the launch traced here: 233 us
  Pallas kernels  152 us (65%)
  local copies, waits for them, and re-layouts  30.6 us (13%)
  starting transfers between devices  26.1 us (11%)
  waiting for transfers between devices  21.4 us (9%)
    pallas_call x2, Pallas kernels, translate(): pl.pallas_call(functools.partial(translate_kernel, group, count, scale, f...  136 us
    optimization_barrier x1, local copies, waits for them, and re-layouts, local(): lax.optimization_barrier((outgoing, near, m2l_matrices, leaf_source, coar...  21.1 us
    all_to_all x1, waiting for transfers between devices, local(): lax.all_to_all(outgoing, ('wide', 'narrow'), split_axis=0, concat_axis=0,...  20.2 us
    pallas_call x1, Pallas kernels, pick_rows(): pl.pallas_call(functools.partial(pick_kernel, capacity), grid=(devices //...  16.2 us
    all_to_all x1, starting transfers between devices, local(): lax.all_to_all(outgoing, ('wide', 'narrow'), split_axis=0, concat_axis=0,...  13.7 us
    all_to_all x1, starting transfers between devices, local(): lax.all_to_all(jnp.broadcast_to(three, (narrow,) + three.shape), 'narrow'...  6.09 us
    unnamed x18, local copies, waits for them, and re-layouts  5.26 us
    ppermute x1, starting transfers between devices, local(): before = lax.ppermute(own, 'wide', up)  5 us
  transfers between devices with their start and end apart: 4, of which 2 were waited for; matrix products, arithmetic and copies ran while one was open for 11% of the time, Pallas kernels for 16%

profile of v3, /device:TPU:1, one launch (start us, length us, event | category | flops | bytes accessed | tf_op | source)
XLA Modules:
  0.0 232.6 jit_solution(12309063859310675859)
XLA Ops:
  0.6 0.0 copy-start
  0.6 0.0 copy-start.6
  0.7 1.2 copy.21
  1.8 0.4 reshape.33
  2.2 0.0 copy-done
  2.2 0.4 convolution_convert_fusion
  2.6 0.0 copy-start.3
  2.6 0.1 copy.22
  2.7 1.3 collective-permute-start.1
  4.0 5.0 %collective-permute-start = (bf16[192,128]{1,0:T(8,128)(2,1)S(1)}, bf16[192,128]{1,0:T(8,128)(2,1)S(1)}, u32[]{:S(2)}, u32[]{:S(2)}) collective-permute-start(bf16[192,128]{1,0:T(8,128)(2,1)S(1)} %reshape.35), channel_id=1, source_target_pairs={{0,8},{8,16},{16,24},{24,32},{32,40},{40,48},{48,56},{56,64},{64,7... | collective-permute-start | bytes 147464 | tf_op jit(solution)/shard_map/ppermute | solution.py:228
  9.1 0.0 collective-permute-done.1
  9.1 1.1 collective-permute-done
  10.2 1.2 broadcast_in_dim.7
  11.4 6.1 %all-to-all-start = ((bf16[8,576,128]{2,1,0:T(8,128)(2,1)}), bf16[8,576,128]{2,1,0:T(8,128)(2,1)S(1)}, u32[]{:S(2)}, u32[]{:S(2)}) async-start(bf16[8,576,128]{2,1,0:T(8,128)(2,1)} %broadcast_in_dim.7), calls=%async_computation | async-start | bytes 2359296 | tf_op jit(solution)/shard_map/all_to_all | solution.py:231
  17.5 0.1 pad.12.clone
  17.6 0.9 reshape.32.cells_ref.refs_0_
  18.4 0.0 copy-done.6
  18.5 0.6 multiply_bitcast_fusion.idx_hbm
  19.1 16.2 %shard_map.85 = bf16[128,160,128]{2,1,0:T(8,128)(2,1)} custom-call(s32[128,128]{1,0:T(8,128)} %multiply_bitcast_fusion.idx_hbm, bf16[1536,128]{1,0:T(8,128)(2,1)} %reshape.32.cells_ref.refs_0_), custom_call_target="tpu_custom_call" | custom-call | bytes 33554432 | tf_op jit(solution)/shard_map/pallas_call | solution.py:186
  35.2 0.0 copy-done.3
  35.3 0.0 all-to-all-done
  35.3 0.0 copy-start.1
  35.3 0.0 copy-start.4
  35.3 0.0 copy-start.2
  35.3 1.1 copy-done.1
  36.4 13.7 %all-to-all-start.1 = ((bf16[128,160,128]{2,1,0:T(8,128)(2,1)}), bf16[128,160,128]{2,1,0:T(8,128)(2,1)}, u32[]{:S(2)}, u32[]{:S(2)}) async-start(bf16[128,160,128]{2,1,0:T(8,128)(2,1)} %shard_map.85), calls=%async_computation.1 | async-start | bytes 10485760 | tf_op jit(solution)/shard_map/all_to_all | solution.py:240
  50.1 0.0 copy-done.4
  50.1 0.2 fusion.5
  50.4 0.1 reshape.38
  50.5 0.7 reshape.39.idx_hbm
  51.1 0.0 copy-done.2
  51.1 0.1 add_select_fusion
  51.2 1.0 reshape.37.idx_hbm
  52.2 21.1 %copy.17.m2l_ref = bf16[189,152,152]{2,1,0:T(8,128)(2,1)} copy(bf16[189,152,152]{0,2,1:T(8,128)(2,1)} %param.7) | data formatting | bytes 17466624 | tf_op jit(solution)/shard_map/optimization_barrier | solution.py:237
  73.3 21.2 %shard_map.86 = f32[96,152]{1,0:T(8,128)} custom-call(s32[21,7,128]{2,1,0:T(8,128)} %reshape.39.idx_hbm, bf16[189,152,152]{2,1,0:T(8,128)(2,1)} %copy.17.m2l_ref, bf16[4608,128]{1,0:T(8,128)(2,1)} %bitcast.7), custom_call_target="tpu_custom_call" | custom-call | flops 7134511104 | bytes 20971520 | tf_op jit(solution)/shard_map/pallas_call | solution.py:129
  94.5 0.0 copy-start.5
  94.5 20.2 %all-to-all-done.1.refs_1_ = bf16[128,160,128]{2,1,0:T(8,128)(2,1)} async-done(((bf16[128,160,128]{2,1,0:T(8,128)(2,1)}), bf16[128,160,128]{2,1,0:T(8,128)(2,1)}, u32[]{:S(2)}, u32[]{:S(2)}) %all-to-all-start.1) | async-done | bytes 5242912 | tf_op jit(solution)/shard_map/all_to_all | solution.py:240
  114.7 115.0 %shard_map.87 = f32[768,152]{1,0:T(8,128)} custom-call(s32[189,6,128]{2,1,0:T(8,128)} %reshape.37.idx_hbm, bf16[189,152,152]{2,1,0:T(8,128)(2,1)} %copy.17.m2l_ref, bf16[1536,128]{1,0:T(8,128)(2,1)} %reshape.32.cells_ref.refs_0_, bf16[128,160,128]{2,1,0:T(8,128)(2,1)} %all-to-all-done.1.refs_1_), custom_call_target="tpu_custom_call" | custom-call | flops 57076088832 | bytes 20971520 | tf_op jit(solution)/shard_map/pallas_call | solution.py:129
  229.7 2.1 copy.19
  231.9 0.0 copy-done.5
  231.9 0.7 copy.20
  (4 shorter events, 0.1 us)
Async XLA Ops:
  0.6 1.6 copy-start
  0.6 17.8 %copy-start.6 = (s32[1,128,128]{2,1,0:T(8,128)S(1)}, s32[1,128,128]{2,1,0:T(8,128)}, u32[]{:S(2)}) copy-start(s32[1,128,128]{2,1,0:T(8,128)} %param.9) | copy-start | bytes 196612
  2.6 32.7 %copy-start.3 = (bf16[96,152]{0,1:T(8,128)(2,1)}, bf16[96,152]{0,1:T(8,128)(2,1)S(1)}, u32[]{:S(2)}) copy-start(bf16[96,152]{0,1:T(8,128)(2,1)S(1)} %convolution_convert_fusion) | copy-start | bytes 87556
  2.7 6.3 %collective-permute-start.1 = (bf16[192,128]{1,0:T(8,128)(2,1)S(1)}, bf16[192,128]{1,0:T(8,128)(2,1)S(1)}, u32[]{:S(2)}, u32[]{:S(2)}) collective-permute-start(bf16[192,128]{1,0:T(8,128)(2,1)S(1)} %reshape.35), channel_id=1, source_target_pairs={{8,0},{16,8},{24,16},{32,24},{40,32},{48,40},{56,48},{64,56},{72,6... | collective-permute-start | bytes 147464 | tf_op jit(solution)/shard_map/ppermute | solution.py:229
  4.0 6.2 %collective-permute-start = (bf16[192,128]{1,0:T(8,128)(2,1)S(1)}, bf16[192,128]{1,0:T(8,128)(2,1)S(1)}, u32[]{:S(2)}, u32[]{:S(2)}) collective-permute-start(bf16[192,128]{1,0:T(8,128)(2,1)S(1)} %reshape.35), channel_id=1, source_target_pairs={{0,8},{8,16},{16,24},{24,32},{32,40},{40,48},{48,56},{56,64},{64,7... | collective-permute-start | bytes 147464 | tf_op jit(solution)/shard_map/ppermute | solution.py:228
  11.4 23.8 %all-to-all-start = ((bf16[8,576,128]{2,1,0:T(8,128)(2,1)}), bf16[8,576,128]{2,1,0:T(8,128)(2,1)S(1)}, u32[]{:S(2)}, u32[]{:S(2)}) async-start(bf16[8,576,128]{2,1,0:T(8,128)(2,1)} %broadcast_in_dim.7), calls=%async_computation | async-start | bytes 2359296 | tf_op jit(solution)/shard_map/all_to_all | solution.py:231
  35.3 1.1 copy-start.1
  35.3 14.9 %copy-start.4 = (s32[189,96]{1,0:T(8,128)S(1)}, s32[189,96]{1,0:T(8,128)}, u32[]{:S(2)}) copy-start(s32[189,96]{1,0:T(8,128)} %param.11) | copy-start | bytes 217732
  35.3 15.8 %copy-start.2 = (s32[189,768]{1,0:T(8,128)S(1)}, s32[189,768]{1,0:T(8,128)}, u32[]{:S(2)}) copy-start(s32[189,768]{1,0:T(8,128)} %param.10) | copy-start | bytes 1741828
  36.4 78.4 %all-to-all-start.1 = ((bf16[128,160,128]{2,1,0:T(8,128)(2,1)}), bf16[128,160,128]{2,1,0:T(8,128)(2,1)}, u32[]{:S(2)}, u32[]{:S(2)}) async-start(bf16[128,160,128]{2,1,0:T(8,128)(2,1)} %shard_map.85), calls=%async_computation.1 | async-start | bytes 10485760 | tf_op jit(solution)/shard_map/all_to_all | solution.py:240
  94.5 137.4 %copy-start.5 = (f32[96,152]{1,0:T(8,128)S(1)}, f32[96,152]{1,0:T(8,128)}, u32[]{:S(2)}) copy-start(f32[96,152]{1,0:T(8,128)} %shard_map.86) | copy-start | bytes 175108

commit v4 on v3

--- a/solution.py
+++ b/solution.py
@@ -107,7 +107,8 @@
     @pl.when(step == steps - 1)
     def _():
         multiply((burst - 1) % RING, 0, count)
-        out_ref[...] = scale * acc[:, 0:width] if scale != 1 else acc[:, 0:width]
+        total_t = acc[...].T[0:width]
+        out_ref[...] = scale * total_t if scale != 1 else total_t
 
 
 def translate(idx, m2l, near2, far, group, count, scale, burst, pieces):
@@ -130,8 +131,8 @@
         functools.partial(translate_kernel, group, count, scale, far is not None, burst, pieces),
         grid=(noff // (burst * group),),
         in_specs=in_specs,
-        out_specs=pl.BlockSpec((count, width), lambda s: (0, 0)),
-        out_shape=jax.ShapeDtypeStruct((count, width), jnp.float32),
+        out_specs=pl.BlockSpec((width, count), lambda s: (0, 0)),
+        out_shape=jax.ShapeDtypeStruct((width, count), jnp.float32),
         scratch_shapes=[
             pltpu.VMEM((rows, LANES), jnp.float32),
             pltpu.VMEM((count, 2 * LANES), jnp.float32),
@@ -143,10 +144,11 @@
         compiler_params=pltpu.CompilerParams(vmem_limit_bytes=56 * 2**20),
         cost_estimate=pl.CostEstimate(
             flops=2 * noff * count * 256 * 256 * 3, bytes_accessed=20 * 2**20, transcendentals=0),
-    )(*operands)
-
-
-def pick_kernel(capacity, idx_hbm, cells_ref, out_ref, table, f0, f1, s0, s1, sem):
+    )(*operands).T
+
+
+def pick_kernel(capacity, first, idx_hbm, cells_ref, *refs):
+    out_ref, table, f0, f1, s0, s1, sem = refs[-7:]
     step = pl.program_id(0)
     steps = pl.num_programs(0)
     rows_f, smem = (f0, f1), (s0, s1)
@@ -154,7 +156,7 @@
     rows, lane = capacity // SPLIT, LANES // SPLIT
 
     def fetch(k, s):
-        return pltpu.make_async_copy(idx_hbm.at[pl.ds((2 * s + k) * lines, lines)], smem[k], sem.at[k])
+        return pltpu.make_async_copy(idx_hbm.at[pl.ds((2 * (first + s) + k) * lines, lines)], smem[k], sem.at[k])
 
     @pl.when(step == 0)
     def _():
@@ -180,25 +182,30 @@
             fetch(k, step + 1).start()
 
 
-def pick_rows(leaf2, chosen):
+def pick_rows(leaf2, chosen, half, partial=None):
     devices, capacity = chosen.shape
     lines = 8
+    steps = devices // (4 * lines)
+    first = half * steps
+    operands = [chosen, leaf2]
+    in_specs = [pl.BlockSpec(memory_space=pl.ANY), pl.BlockSpec(leaf2.shape, lambda s: (0, 0))]
+    if partial is not None:
+        operands.append(partial)
+        in_specs.append(pl.BlockSpec(memory_space=pl.ANY))
     return pl.pallas_call(
-        functools.partial(pick_kernel, capacity),
-        grid=(devices // (2 * lines),),
-        in_specs=[
-            pl.BlockSpec(memory_space=pl.ANY),
-            pl.BlockSpec(leaf2.shape, lambda s: (0, 0)),
-        ],
-        out_specs=pl.BlockSpec((2 * lines, capacity + capacity // SPLIT, LANES), lambda s: (s, 0, 0)),
+        functools.partial(pick_kernel, capacity, first),
+        grid=(steps,),
+        in_specs=in_specs,
+        out_specs=pl.BlockSpec((2 * lines, capacity + capacity // SPLIT, LANES), lambda s: (first + s, 0, 0)),
         out_shape=jax.ShapeDtypeStruct((devices, capacity + capacity // SPLIT, LANES), jnp.bfloat16),
         scratch_shapes=[pltpu.VMEM(leaf2.shape, jnp.float32)]
         + [pltpu.VMEM((2 * lines * capacity, LANES), jnp.float32)] * 2
         + [pltpu.SMEM((lines, capacity), jnp.int32)] * 2
         + [pltpu.SemaphoreType.DMA((2,))],
+        input_output_aliases={} if partial is None else {2: 0},
         compiler_params=pltpu.CompilerParams(vmem_limit_bytes=56 * 2**20),
-        cost_estimate=pl.CostEstimate(flops=0, bytes_accessed=32 * 2**20, transcendentals=0),
-    )(2 * chosen, leaf2)
+        cost_estimate=pl.CostEstimate(flops=0, bytes_accessed=24 * 2**20, transcendentals=0),
+    )(*operands)
 
 
 def two_rows(x):
@@ -223,27 +230,27 @@
         preferred_element_type=jnp.float32,
     ).astype(jnp.bfloat16)
     own = two_rows(parents)
+    group = lax.all_to_all(
+        jnp.broadcast_to(own, (narrow,) + own.shape), "narrow", split_axis=0, concat_axis=0, tiled=True
+    ).reshape(narrow * own.shape[0], LANES)
+
+    leaf2 = two_rows(leaf_density)
+    chosen = 2 * send_index[0]
+    outgoing = pick_rows(leaf2, chosen, 0)
+    outgoing, group = lax.optimization_barrier((outgoing, group))
     up = [(i, i + 1) for i in range(wide - 1)]
     down = [(j, i) for i, j in up]
-    before = lax.ppermute(own, "wide", up)
-    after = lax.ppermute(own, "wide", down)
-    three = jnp.concatenate([before, own, after], axis=0)
-    near = lax.all_to_all(
-        jnp.broadcast_to(three, (narrow,) + three.shape), "narrow", split_axis=0, concat_axis=0, tiled=True
-    ).reshape(narrow * three.shape[0], LANES)
-
-    leaf2 = two_rows(leaf_density)
-    outgoing = pick_rows(leaf2, send_index[0])
-    outgoing, near, m2l_matrices, leaf_source, coarse_source = lax.optimization_barrier(
-        (outgoing, near, m2l_matrices, leaf_source, coarse_source)
+    before = lax.ppermute(group, "wide", up)
+    after = lax.ppermute(group, "wide", down)
+    outgoing = pick_rows(leaf2, chosen, 1, outgoing)
+    outgoing, before, after, m2l_matrices, leaf_source, coarse_source = lax.optimization_barrier(
+        (outgoing, before, after, m2l_matrices, leaf_source, coarse_source)
     )
     far = lax.all_to_all(outgoing, ("wide", "narrow"), split_axis=0, concat_axis=0, tiled=True)
 
-    group_rows = narrow * parents_here
-    rel = coarse_source - (lax.axis_index("wide") - 1) * group_rows
-    group, inside = rel // group_rows, rel % group_rows
-    slot = (inside // parents_here) * (3 * parents_here) + group * parents_here + inside % parents_here
-    coarse_row = jnp.where(coarse_source < 0, 0, ZERO + 2 * slot)
+    near = jnp.concatenate([before, group, after], axis=0)
+    base = (lax.axis_index("wide") - 1) * (narrow * parents_here)
+    coarse_row = jnp.where(coarse_source < 0, 0, ZERO + 2 * (coarse_source - base))
     together = 9
     coarse_index = lines_of(coarse_row.reshape(noff // together, together * parents_here))
     coarse_local = translate(coarse_index, m2l_matrices, near, None, together, parents_here, 0.5, 3, 1)

time: 234 us -> 230 us (0.983)
  local copies, waits for them, and re-layouts: 30.6 us -> 26.2 us
  Pallas kernels: 152 us -> 155 us
    unnamed x18 -> x12, local copies, waits for them, and re-layouts: 5.26 us -> 1.3 us
    pallas_call x1 -> x2, Pallas kernels: 16.2 us -> 18.8 us  [pick_rows(): pl.pallas_call(functools.partial(pick_kernel, capacity, first), grid=(ste...]
  transfers between devices with their start and end apart: 4 -> 4, of which waited for: 2 -> 1; matrix products, arithmetic and copies ran while one was open for 11% -> 11% of each run, Pallas kernels for 16% -> 18%
where the time goes in v4:
time: 230 us; the launch traced here: 229 us
  Pallas kernels  155 us (67%)
  local copies, waits for them, and re-layouts  26.2 us (11%)
  starting transfers between devices  24.7 us (11%)
  waiting for transfers between devices  19.2 us (8%)
    pallas_call x2, Pallas kernels, translate(): pl.pallas_call(functools.partial(translate_kernel, group, count, scale, f...  136 us
    optimization_barrier x1, local copies, waits for them, and re-layouts, local(): lax.optimization_barrier((outgoing, before, after, m2l_matrices, leaf_sou...  21.1 us
    all_to_all x1, waiting for transfers between devices, local(): lax.all_to_all(outgoing, ('wide', 'narrow'), split_axis=0, concat_axis=0,...  19.2 us
    pallas_call x2, Pallas kernels, pick_rows(): pl.pallas_call(functools.partial(pick_kernel, capacity, first), grid=(ste...  18.8 us
    all_to_all x1, starting transfers between devices, local(): lax.all_to_all(outgoing, ('wide', 'narrow'), split_axis=0, concat_axis=0,...  13.2 us
    all_to_all x1, starting transfers between devices, local(): lax.all_to_all(jnp.broadcast_to(own, (narrow,) + own.shape), 'narrow', sp...  5.97 us
  transfers between devices with their start and end apart: 4, of which 1 were waited for; matrix products, arithmetic and copies ran while one was open for 11% of the time, Pallas kernels for 18%

profile of v4, /device:TPU:1, one launch (start us, length us, event | category | flops | bytes accessed | tf_op | source)
XLA Modules:
  0.0 228.5 jit_solution(9902186993874695462)
XLA Ops:
  0.6 0.0 copy-start
  0.6 1.2 copy.18
  1.8 0.0 copy-start.4
  1.8 0.4 reshape.33
  2.2 0.0 copy-done
  2.2 0.4 convolution_convert_fusion
  2.6 0.0 copy-start.2
  2.6 0.1 copy.19
  2.7 0.8 broadcast_in_dim.7
  3.5 6.0 %all-to-all-start = ((bf16[8,192,128]{2,1,0:T(8,128)(2,1)}), bf16[8,192,128]{2,1,0:T(8,128)(2,1)S(1)}, u32[]{:S(2)}, u32[]{:S(2)}) async-start(bf16[8,192,128]{2,1,0:T(8,128)(2,1)} %broadcast_in_dim.7), calls=%async_computation | async-start | bytes 786432 | tf_op jit(solution)/shard_map/all_to_all | solution.py:233
  9.5 0.1 pad.12.clone
  9.6 0.9 reshape.32.cells_ref.refs_0_
  10.5 0.0 copy-done.4
  10.5 0.6 multiply_bitcast_fusion.idx_hbm
  11.1 9.4 %shard_map.85.refs_0_ = bf16[128,160,128]{2,1,0:T(8,128)(2,1)} custom-call(s32[128,128]{1,0:T(8,128)} %multiply_bitcast_fusion.idx_hbm, bf16[1536,128]{1,0:T(8,128)(2,1)} %reshape.32.cells_ref.refs_0_), custom_call_target="tpu_custom_call" | custom-call | bytes 25165824 | tf_op jit(solution)/shard_map/pallas_call | solution.py:195
  20.5 0.0 copy-done.2
  20.5 0.0 all-to-all-done
  20.5 1.3 collective-permute-start.1
  21.8 4.2 %collective-permute-start = (bf16[1536,128]{1,0:T(8,128)(2,1)S(1)}, bf16[1536,128]{1,0:T(8,128)(2,1)S(1)}, u32[]{:S(2)}, u32[]{:S(2)}) collective-permute-start(bf16[1536,128]{1,0:T(8,128)(2,1)S(1)} %bitcast.10), channel_id=1, source_target_pairs={{0,8},{8,16},{16,24},{24,32},{32,40},{40,48},{48,56},{56,64},{64,7... | collective-permute-start | bytes 1179656 | tf_op jit(solution)/shard_map/ppermute | solution.py:243
  26.1 9.4 %shard_map.86 = bf16[128,160,128]{2,1,0:T(8,128)(2,1)} custom-call(s32[128,128]{1,0:T(8,128)} %multiply_bitcast_fusion.idx_hbm, bf16[1536,128]{1,0:T(8,128)(2,1)} %reshape.32.cells_ref.refs_0_, bf16[128,160,128]{2,1,0:T(8,128)(2,1)} %shard_map.85.refs_0_), custom_call_target="tpu_custom_call", output_to_operand_aliasing={{}: (2, {})} | custom-call | bytes 25165824 | tf_op jit(solution)/shard_map/pallas_call | solution.py:195
  35.5 0.0 copy-start.3
  35.5 0.0 copy-start.1
  35.6 0.0 collective-permute-done.1
  35.6 0.0 collective-permute-done
  35.6 13.2 %all-to-all-start.1 = ((bf16[128,160,128]{2,1,0:T(8,128)(2,1)}), bf16[128,160,128]{2,1,0:T(8,128)(2,1)}, u32[]{:S(2)}, u32[]{:S(2)}) async-start(bf16[128,160,128]{2,1,0:T(8,128)(2,1)} %shard_map.86), calls=%async_computation.1 | async-start | bytes 10485760 | tf_op jit(solution)/shard_map/all_to_all | solution.py:249
  48.8 0.0 copy-done.3
  48.8 0.1 reshape.38
  48.9 0.7 reshape.39.idx_hbm
  49.6 0.0 copy-done.1
  49.6 0.1 add_select_fusion
  49.7 1.0 reshape.37.idx_hbm
  50.6 21.1 %copy.16.m2l_ref = bf16[189,152,152]{2,1,0:T(8,128)(2,1)} copy(bf16[189,152,152]{0,2,1:T(8,128)(2,1)} %param.7) | data formatting | bytes 17466624 | tf_op jit(solution)/shard_map/optimization_barrier | solution.py:246
  71.7 1.2 pad_maximum_fusion.refs_0_
  72.9 21.3 %shard_map.87 = f32[152,96]{1,0:T(8,128)} custom-call(s32[21,7,128]{2,1,0:T(8,128)} %reshape.39.idx_hbm, bf16[189,152,152]{2,1,0:T(8,128)(2,1)} %copy.16.m2l_ref, bf16[4608,128]{1,0:T(8,128)(2,1)} %pad_maximum_fusion.refs_0_), custom_call_target="tpu_custom_call" | custom-call | flops 7134511104 | bytes 20971520 | tf_op jit(solution)/shard_map/pallas_call | solution.py:130
  94.2 19.2 %all-to-all-done.1.refs_1_ = bf16[128,160,128]{2,1,0:T(8,128)(2,1)} async-done(((bf16[128,160,128]{2,1,0:T(8,128)(2,1)}), bf16[128,160,128]{2,1,0:T(8,128)(2,1)}, u32[]{:S(2)}, u32[]{:S(2)}) %all-to-all-start.1) | async-done | bytes 5242912 | tf_op jit(solution)/shard_map/all_to_all | solution.py:249
  113.4 115.0 %shard_map.88 = f32[152,768]{1,0:T(8,128)} custom-call(s32[189,6,128]{2,1,0:T(8,128)} %reshape.37.idx_hbm, bf16[189,152,152]{2,1,0:T(8,128)(2,1)} %copy.16.m2l_ref, bf16[1536,128]{1,0:T(8,128)(2,1)} %reshape.32.cells_ref.refs_0_, bf16[128,160,128]{2,1,0:T(8,128)(2,1)} %all-to-all-done.1.refs_1_), custom_call_target="tpu_custom_call" | custom-call | flops 57076088832 | bytes 20971520 | tf_op jit(solution)/shard_map/pallas_call | solution.py:130
  (4 shorter events, 0.1 us)
Async XLA Ops:
  0.6 1.6 copy-start
  1.8 8.7 %copy-start.4 = (s32[1,128,128]{2,1,0:T(8,128)S(1)}, s32[1,128,128]{2,1,0:T(8,128)}, u32[]{:S(2)}) copy-start(s32[1,128,128]{2,1,0:T(8,128)} %param.9) | copy-start | bytes 196612
  2.6 17.9 %copy-start.2 = (bf16[96,152]{0,1:T(8,128)(2,1)}, bf16[96,152]{0,1:T(8,128)(2,1)S(1)}, u32[]{:S(2)}) copy-start(bf16[96,152]{0,1:T(8,128)(2,1)S(1)} %convolution_convert_fusion) | copy-start | bytes 87556
  3.5 17.0 %all-to-all-start = ((bf16[8,192,128]{2,1,0:T(8,128)(2,1)}), bf16[8,192,128]{2,1,0:T(8,128)(2,1)S(1)}, u32[]{:S(2)}, u32[]{:S(2)}) async-start(bf16[8,192,128]{2,1,0:T(8,128)(2,1)} %broadcast_in_dim.7), calls=%async_computation | async-start | bytes 786432 | tf_op jit(solution)/shard_map/all_to_all | solution.py:233
  20.5 15.0 %collective-permute-start.1 = (bf16[1536,128]{1,0:T(8,128)(2,1)S(1)}, bf16[1536,128]{1,0:T(8,128)(2,1)S(1)}, u32[]{:S(2)}, u32[]{:S(2)}) collective-permute-start(bf16[1536,128]{1,0:T(8,128)(2,1)S(1)} %bitcast.9), channel_id=1, source_target_pairs={{8,0},{16,8},{24,16},{32,24},{40,32},{48,40},{56,48},{64,56},{72,6... | collective-permute-start | bytes 1179656 | tf_op jit(solution)/shard_map/ppermute | solution.py:244
  21.8 13.7 %collective-permute-start = (bf16[1536,128]{1,0:T(8,128)(2,1)S(1)}, bf16[1536,128]{1,0:T(8,128)(2,1)S(1)}, u32[]{:S(2)}, u32[]{:S(2)}) collective-permute-start(bf16[1536,128]{1,0:T(8,128)(2,1)S(1)} %bitcast.10), channel_id=1, source_target_pairs={{0,8},{8,16},{16,24},{24,32},{32,40},{40,48},{48,56},{56,64},{64,7... | collective-permute-start | bytes 1179656 | tf_op jit(solution)/shard_map/ppermute | solution.py:243
  35.5 13.3 %copy-start.3 = (s32[189,96]{1,0:T(8,128)S(1)}, s32[189,96]{1,0:T(8,128)}, u32[]{:S(2)}) copy-start(s32[189,96]{1,0:T(8,128)} %param.11) | copy-start | bytes 217732
  35.5 14.0 %copy-start.1 = (s32[189,768]{1,0:T(8,128)S(1)}, s32[189,768]{1,0:T(8,128)}, u32[]{:S(2)}) copy-start(s32[189,768]{1,0:T(8,128)} %param.10) | copy-start | bytes 1741828
  35.6 77.8 %all-to-all-start.1 = ((bf16[128,160,128]{2,1,0:T(8,128)(2,1)}), bf16[128,160,128]{2,1,0:T(8,128)(2,1)}, u32[]{:S(2)}, u32[]{:S(2)}) async-start(bf16[128,160,128]{2,1,0:T(8,128)(2,1)} %shard_map.86), calls=%async_computation.1 | async-start | bytes 10485760 | tf_op jit(solution)/shard_map/all_to_all | solution.py:249

commit v5 on v4

--- a/solution.py
+++ b/solution.py
@@ -32,8 +32,8 @@
     if packed:
         far_hbm, refs = refs[0], refs[1:]
     out_ref, table, acc, idx_vmem = refs[:4]
-    rows_f, mats, smem = refs[4:7], refs[7:10], refs[10:13]
-    sem, vsem = refs[13:15]
+    rows_f, kept, smem = refs[4:7], refs[7], refs[8:11]
+    sem, vsem = refs[11:13]
     step = pl.program_id(0)
     steps = pl.num_programs(0)
     width = m2l_ref.shape[1]
@@ -47,24 +47,24 @@
             i = smem[k][t // LANES, t % LANES]
             rows_f[k][pl.ds(2 * t, 2), :] = table[pl.ds(i, 2), :]
 
-    def multiply(k, lo, hi):
+    def multiply(k, lo, hi, matrix):
         sides = []
         for g in range(group):
             for side in range(2):
                 rows = pl.ds(2 * (g * count + lo) + side, hi - lo, stride=2)
                 sides.append(rows_f[k][rows, :].astype(jnp.bfloat16))
-        acc[lo:hi] += jnp.dot(jnp.concatenate(sides, axis=1), mats[k][...], preferred_element_type=jnp.float32)
-
-    def load_matrix(k, c):
-        for g in range(group):
-            mats[k][2 * LANES * g:2 * LANES * g + width, 0:width] = m2l_ref[c * group + g]
+        acc[lo:hi] += jnp.dot(jnp.concatenate(sides, axis=1), matrix, preferred_element_type=jnp.float32)
+
+    def matrix_of(c):
+        room = 2 * LANES - width
+        return jnp.concatenate([jnp.pad(m2l_ref[c * group + g], ((0, room), (0, room))) for g in range(group)], axis=0)
 
     @pl.when(step == 0)
     def _():
         copy = pltpu.make_async_copy(idx_hbm, idx_vmem, vsem)
         copy.start()
         if packed:
-            far, fsem = refs[15:17]
+            far, fsem = refs[13:15]
             span = far.shape[0] // PARTS
 
             def part(q):
@@ -75,11 +75,17 @@
         acc[...] = jnp.zeros_like(acc)
         last = rows_f[(burst - 1) % RING]
         last[...] = jnp.zeros_like(last)
-        for w in mats:
-            w[...] = jnp.zeros_like(w)
+        kept[...] = jnp.zeros_like(kept)
         table[0:ZERO, :] = jnp.zeros((ZERO, LANES), jnp.float32)
+        copy.wait()
+        for k in range(RING):
+            fetch(k, k).start()
         n = near_ref.shape[0]
-        table[pl.ds(ZERO, n), :] = near_ref[...].astype(jnp.float32)
+        if packed:
+            place_cells(near_ref[...], table, ZERO)
+            n = 2 * n
+        else:
+            table[pl.ds(ZERO, n), :] = near_ref[...].astype(jnp.float32)
         if packed:
             for q in range(PARTS):
                 part(q).wait()
@@ -88,32 +94,31 @@
                 def _(b):
                     p = q * span + b
                     place_far(far[p], table, pl.multiple_of(ZERO + n + p * 2 * (far.shape[1] - LANES // SPLIT), 8))
-        copy.wait()
-        for k in range(RING):
-            fetch(k, k).start()
 
     for c in range(burst):
         k = c % RING
         fetch(k, burst * step + c).wait()
-        load_matrix(k, c)
+        matrix = kept[...] if c == 0 else matrix_of(c - 1)
         for p in range(pieces):
             gather(k, total * p // pieces, total * (p + 1) // pieces)
-            multiply((c + burst - 1) % burst % RING, count * p // pieces, count * (p + 1) // pieces)
+            multiply((c + burst - 1) % burst % RING, count * p // pieces, count * (p + 1) // pieces, matrix)
 
         @pl.when(burst * step + c + RING < burst * steps)
         def _():
             fetch(k, burst * step + c + RING).start()
 
+    kept[...] = matrix_of(burst - 1)
+
     @pl.when(step == steps - 1)
     def _():
-        multiply((burst - 1) % RING, 0, count)
+        multiply((burst - 1) % RING, 0, count, kept[...])
         total_t = acc[...].T[0:width]
         out_ref[...] = scale * total_t if scale != 1 else total_t
 
 
 def translate(idx, m2l, near2, far, group, count, scale, burst, pieces):
     noff, width, _ = m2l.shape
-    rows = ZERO + near2.shape[0]
+    rows = ZERO + near2.shape[0] * (1 if far is None else 2)
     total = group * count
     operands = [idx, m2l, near2]
     in_specs = [
@@ -138,7 +143,7 @@
             pltpu.VMEM((count, 2 * LANES), jnp.float32),
             pltpu.VMEM(idx.shape, jnp.int32),
         ] + [pltpu.VMEM((2 * total, LANES), jnp.float32)] * RING
-        + [pltpu.VMEM((group * 2 * LANES, 2 * LANES), jnp.bfloat16)] * RING
+        + [pltpu.VMEM((group * 2 * LANES, 2 * LANES), jnp.bfloat16)]
         + [pltpu.SMEM(idx.shape[1:], jnp.int32)] * RING
         + [pltpu.SemaphoreType.DMA((RING,)), pltpu.SemaphoreType.DMA] + extra,
         compiler_params=pltpu.CompilerParams(vmem_limit_bytes=56 * 2**20),
@@ -147,8 +152,15 @@
     )(*operands).T
 
 
-def pick_kernel(capacity, first, idx_hbm, cells_ref, *refs):
-    out_ref, table, f0, f1, s0, s1, sem = refs[-7:]
+def place_cells(cells, table, base):
+    count, width = cells.shape
+    table[pl.ds(base, count, stride=2), :] = cells[:, 0:LANES].astype(jnp.float32)
+    rest = jnp.pad(cells[:, LANES:width].astype(jnp.float32), ((0, 0), (0, 2 * LANES - width)))
+    table[pl.ds(base + 1, count, stride=2), :] = rest
+
+
+def pick_kernel(capacity, first, idx_ref, cells_ref, *refs):
+    out_ref, table, twice, f0, f1, s0, s1, sem = refs[-8:]
     step = pl.program_id(0)
     steps = pl.num_programs(0)
     rows_f, smem = (f0, f1), (s0, s1)
@@ -156,13 +168,14 @@
     rows, lane = capacity // SPLIT, LANES // SPLIT
 
     def fetch(k, s):
-        return pltpu.make_async_copy(idx_hbm.at[pl.ds((2 * (first + s) + k) * lines, lines)], smem[k], sem.at[k])
+        return pltpu.make_async_copy(twice.at[pl.ds((2 * (first + s) + k) * lines, lines)], smem[k], sem.at[k])
 
     @pl.when(step == 0)
     def _():
+        twice[...] = 2 * idx_ref[...]
         for k in range(2):
             fetch(k, 0).start()
-        table[...] = cells_ref[...].astype(jnp.float32)
+        place_cells(cells_ref[...], table, 0)
 
     for k in range(2):
         fetch(k, step).wait()
@@ -182,13 +195,13 @@
             fetch(k, step + 1).start()
 
 
-def pick_rows(leaf2, chosen, half, partial=None):
+def pick_rows(cells, chosen, half, partial=None):
     devices, capacity = chosen.shape
     lines = 8
     steps = devices // (4 * lines)
     first = half * steps
-    operands = [chosen, leaf2]
-    in_specs = [pl.BlockSpec(memory_space=pl.ANY), pl.BlockSpec(leaf2.shape, lambda s: (0, 0))]
+    operands = [chosen, cells]
+    in_specs = [pl.BlockSpec(x.shape, lambda s: (0, 0), pipeline_mode=pl.Buffered(1)) for x in operands]
     if partial is not None:
         operands.append(partial)
         in_specs.append(pl.BlockSpec(memory_space=pl.ANY))
@@ -198,7 +211,7 @@
         in_specs=in_specs,
         out_specs=pl.BlockSpec((2 * lines, capacity + capacity // SPLIT, LANES), lambda s: (first + s, 0, 0)),
         out_shape=jax.ShapeDtypeStruct((devices, capacity + capacity // SPLIT, LANES), jnp.bfloat16),
-        scratch_shapes=[pltpu.VMEM(leaf2.shape, jnp.float32)]
+        scratch_shapes=[pltpu.VMEM((2 * cells.shape[0], LANES), jnp.float32), pltpu.VMEM(chosen.shape, jnp.int32)]
         + [pltpu.VMEM((2 * lines * capacity, LANES), jnp.float32)] * 2
         + [pltpu.SMEM((lines, capacity), jnp.int32)] * 2
         + [pltpu.SemaphoreType.DMA((2,))],
@@ -234,15 +247,14 @@
         jnp.broadcast_to(own, (narrow,) + own.shape), "narrow", split_axis=0, concat_axis=0, tiled=True
     ).reshape(narrow * own.shape[0], LANES)
 
-    leaf2 = two_rows(leaf_density)
-    chosen = 2 * send_index[0]
-    outgoing = pick_rows(leaf2, chosen, 0)
+    chosen = send_index[0]
+    outgoing = pick_rows(leaf_density, chosen, 0)
     outgoing, group = lax.optimization_barrier((outgoing, group))
     up = [(i, i + 1) for i in range(wide - 1)]
     down = [(j, i) for i, j in up]
     before = lax.ppermute(group, "wide", up)
     after = lax.ppermute(group, "wide", down)
-    outgoing = pick_rows(leaf2, chosen, 1, outgoing)
+    outgoing = pick_rows(leaf_density, chosen, 1, outgoing)
     outgoing, before, after, m2l_matrices, leaf_source, coarse_source = lax.optimization_barrier(
         (outgoing, before, after, m2l_matrices, leaf_source, coarse_source)
     )
@@ -259,7 +271,7 @@
         jnp.where(leaf_source < 0, 0, ZERO + 2 * leaf_source).reshape(noff // LEAF_GROUP, LEAF_GROUP * cells)
     )
     far, leaf_index, coarse_local = lax.optimization_barrier((far, leaf_index, coarse_local))
-    leaf_local = translate(leaf_index, m2l_matrices, leaf2, far, LEAF_GROUP, cells, 1, LEAF_BURST, LEAF_PIECES)
+    leaf_local = translate(leaf_index, m2l_matrices, leaf_density, far, LEAF_GROUP, cells, 1, LEAF_BURST, LEAF_PIECES)
     return (leaf_local, parents, coarse_local)
 
 

time: 230 us -> 226 us (0.983)
  Pallas kernels: 155 us -> 152 us
    pallas_call x2, Pallas kernels: 136 us -> 133 us  [translate(): pl.pallas_call(functools.partial(translate_kernel, group, count, scale, f...]
  transfers between devices with their start and end apart: 4 -> 4, of which waited for: 1 -> 1; matrix products, arithmetic and copies ran while one was open for 11% -> 11% of each run, Pallas kernels for 18% -> 17%
where the time goes in v5:
time: 226 us; the launch traced here: 225 us
  Pallas kernels  152 us (67%)
  local copies, waits for them, and re-layouts  25.3 us (11%)
  starting transfers between devices  24.7 us (11%)
  waiting for transfers between devices  20.5 us (9%)
    pallas_call x2, Pallas kernels, translate(): pl.pallas_call(functools.partial(translate_kernel, group, count, scale, f...  133 us
    optimization_barrier x1, local copies, waits for them, and re-layouts, local(): lax.optimization_barrier((outgoing, before, after, m2l_matrices, leaf_sou...  21.1 us
    all_to_all x1, waiting for transfers between devices, local(): lax.all_to_all(outgoing, ('wide', 'narrow'), split_axis=0, concat_axis=0,...  20.5 us
    pallas_call x2, Pallas kernels, pick_rows(): pl.pallas_call(functools.partial(pick_kernel, capacity, first), grid=(ste...  18.7 us
    all_to_all x1, starting transfers between devices, local(): lax.all_to_all(outgoing, ('wide', 'narrow'), split_axis=0, concat_axis=0,...  13.2 us
    all_to_all x1, starting transfers between devices, local(): lax.all_to_all(jnp.broadcast_to(own, (narrow,) + own.shape), 'narrow', sp...  5.97 us
  transfers between devices with their start and end apart: 4, of which 1 were waited for; matrix products, arithmetic and copies ran while one was open for 11% of the time, Pallas kernels for 17%

profile of v5, /device:TPU:1, one launch (start us, length us, event | category | flops | bytes accessed | tf_op | source)
XLA Modules:
  0.0 225.3 jit_solution(15842660003670930251)
XLA Ops:
  0.6 0.0 copy-start
  0.6 1.2 copy.18.cells_ref.refs_0_
  1.8 0.0 copy-start.1
  1.8 0.4 reshape.27
  2.2 0.0 copy-done
  2.2 0.4 convolution_convert_fusion
  2.6 0.0 copy-start.3
  2.6 0.1 copy.22
  2.7 0.8 broadcast_in_dim.7
  3.5 6.0 %all-to-all-start = ((bf16[8,192,128]{2,1,0:T(8,128)(2,1)}), bf16[8,192,128]{2,1,0:T(8,128)(2,1)S(1)}, u32[]{:S(2)}, u32[]{:S(2)}) async-start(bf16[8,192,128]{2,1,0:T(8,128)(2,1)} %broadcast_in_dim.7), calls=%async_computation | async-start | bytes 786432 | tf_op jit(solution)/shard_map/all_to_all | solution.py:246
  9.5 0.0 copy-done.1
  9.5 9.4 %shard_map.85.refs_0_ = bf16[128,160,128]{2,1,0:T(8,128)(2,1)} custom-call(s32[128,128]{1,0:T(8,128)} %bitcast.11, bf16[768,152]{1,0:T(8,128)(2,1)} %copy-done.1), custom_call_target="tpu_custom_call" | custom-call | bytes 25165824 | tf_op jit(solution)/shard_map/pallas_call | solution.py:208
  18.9 0.0 copy-done.3
  18.9 0.0 all-to-all-done
  18.9 1.3 collective-permute-start.1
  20.2 4.2 %collective-permute-start = (bf16[1536,128]{1,0:T(8,128)(2,1)S(1)}, bf16[1536,128]{1,0:T(8,128)(2,1)S(1)}, u32[]{:S(2)}, u32[]{:S(2)}) collective-permute-start(bf16[1536,128]{1,0:T(8,128)(2,1)S(1)} %bitcast.9), channel_id=1, source_target_pairs={{0,8},{8,16},{16,24},{24,32},{32,40},{40,48},{48,56},{56,64},{64,7... | collective-permute-start | bytes 1179656 | tf_op jit(solution)/shard_map/ppermute | solution.py:255
  24.4 9.4 %shard_map.86 = bf16[128,160,128]{2,1,0:T(8,128)(2,1)} custom-call(s32[128,128]{1,0:T(8,128)} %bitcast.12, bf16[768,152]{1,0:T(8,128)(2,1)} %copy-done.1, bf16[128,160,128]{2,1,0:T(8,128)(2,1)} %shard_map.85.refs_0_), custom_call_target="tpu_custom_call", output_to_operand_aliasing={{}: (2, {})} | custom-call | bytes 25165824 | tf_op jit(solution)/shard_map/pallas_call | solution.py:208
  33.8 0.0 copy-start.4
  33.8 0.0 copy-start.2
  33.8 0.0 collective-permute-done.1
  33.8 0.0 collective-permute-done
  33.8 13.2 %all-to-all-start.1 = ((bf16[128,160,128]{2,1,0:T(8,128)(2,1)}), bf16[128,160,128]{2,1,0:T(8,128)(2,1)}, u32[]{:S(2)}, u32[]{:S(2)}) async-start(bf16[128,160,128]{2,1,0:T(8,128)(2,1)} %shard_map.86), calls=%async_computation.1 | async-start | bytes 10485760 | tf_op jit(solution)/shard_map/all_to_all | solution.py:261
  47.1 0.0 copy-done.4
  47.1 0.1 reshape.32
  47.2 0.7 reshape.33.idx_hbm
  47.9 0.0 copy-done.2
  47.9 0.1 add_select_fusion
  48.0 1.0 reshape.31.idx_hbm
  48.9 21.1 %copy.19.m2l_ref = bf16[189,152,152]{2,1,0:T(8,128)(2,1)} copy(bf16[189,152,152]{0,2,1:T(8,128)(2,1)} %param.7) | data formatting | bytes 17466624 | tf_op jit(solution)/shard_map/optimization_barrier | solution.py:258
  70.0 1.2 pad_maximum_fusion.refs_0_
  71.2 20.0 %shard_map.87 = f32[152,96]{1,0:T(8,128)} custom-call(s32[21,7,128]{2,1,0:T(8,128)} %reshape.33.idx_hbm, bf16[189,152,152]{2,1,0:T(8,128)(2,1)} %copy.19.m2l_ref, bf16[4608,128]{1,0:T(8,128)(2,1)} %pad_maximum_fusion.refs_0_), custom_call_target="tpu_custom_call" | custom-call | flops 7134511104 | bytes 20971520 | tf_op jit(solution)/shard_map/pallas_call | solution.py:135
  91.2 20.5 %all-to-all-done.1.refs_1_ = bf16[128,160,128]{2,1,0:T(8,128)(2,1)} async-done(((bf16[128,160,128]{2,1,0:T(8,128)(2,1)}), bf16[128,160,128]{2,1,0:T(8,128)(2,1)}, u32[]{:S(2)}, u32[]{:S(2)}) %all-to-all-start.1) | async-done | bytes 5242912 | tf_op jit(solution)/shard_map/all_to_all | solution.py:261
  111.7 113.4 %shard_map.88 = f32[152,768]{1,0:T(8,128)} custom-call(s32[189,6,128]{2,1,0:T(8,128)} %reshape.31.idx_hbm, bf16[189,152,152]{2,1,0:T(8,128)(2,1)} %copy.19.m2l_ref, bf16[768,152]{1,0:T(8,128)(2,1)} %copy-done.1, bf16[128,160,128]{2,1,0:T(8,128)(2,1)} %all-to-all-done.1.refs_1_), custom_call_target="tpu_custom_call" | custom-call | flops 57076088832 | bytes 20971520 | tf_op jit(solution)/shard_map/pallas_call | solution.py:135
  (4 shorter events, 0.1 us)
Async XLA Ops:
  0.6 1.6 copy-start
  1.8 7.7 %copy-start.1 = (bf16[768,152]{1,0:T(8,128)(2,1)}, bf16[768,152]{1,0:T(8,128)(2,1)S(1)}, u32[]{:S(2)}) copy-start(bf16[768,152]{1,0:T(8,128)(2,1)S(1)} %copy.18.cells_ref.refs_0_) | copy-start | bytes 700420
  2.6 16.3 %copy-start.3 = (bf16[96,152]{0,1:T(8,128)(2,1)}, bf16[96,152]{0,1:T(8,128)(2,1)S(1)}, u32[]{:S(2)}) copy-start(bf16[96,152]{0,1:T(8,128)(2,1)S(1)} %convolution_convert_fusion) | copy-start | bytes 87556
  3.5 15.4 %all-to-all-start = ((bf16[8,192,128]{2,1,0:T(8,128)(2,1)}), bf16[8,192,128]{2,1,0:T(8,128)(2,1)S(1)}, u32[]{:S(2)}, u32[]{:S(2)}) async-start(bf16[8,192,128]{2,1,0:T(8,128)(2,1)} %broadcast_in_dim.7), calls=%async_computation | async-start | bytes 786432 | tf_op jit(solution)/shard_map/all_to_all | solution.py:246
  18.9 14.9 %collective-permute-start.1 = (bf16[1536,128]{1,0:T(8,128)(2,1)S(1)}, bf16[1536,128]{1,0:T(8,128)(2,1)S(1)}, u32[]{:S(2)}, u32[]{:S(2)}) collective-permute-start(bf16[1536,128]{1,0:T(8,128)(2,1)S(1)} %bitcast.8), channel_id=1, source_target_pairs={{8,0},{16,8},{24,16},{32,24},{40,32},{48,40},{56,48},{64,56},{72,6... | collective-permute-start | bytes 1179656 | tf_op jit(solution)/shard_map/ppermute | solution.py:256
  20.2 13.6 %collective-permute-start = (bf16[1536,128]{1,0:T(8,128)(2,1)S(1)}, bf16[1536,128]{1,0:T(8,128)(2,1)S(1)}, u32[]{:S(2)}, u32[]{:S(2)}) collective-permute-start(bf16[1536,128]{1,0:T(8,128)(2,1)S(1)} %bitcast.9), channel_id=1, source_target_pairs={{0,8},{8,16},{16,24},{24,32},{32,40},{40,48},{48,56},{56,64},{64,7... | collective-permute-start | bytes 1179656 | tf_op jit(solution)/shard_map/ppermute | solution.py:255
  33.8 13.3 %copy-start.4 = (s32[189,96]{1,0:T(8,128)S(1)}, s32[189,96]{1,0:T(8,128)}, u32[]{:S(2)}) copy-start(s32[189,96]{1,0:T(8,128)} %param.11) | copy-start | bytes 217732
  33.8 14.1 %copy-start.2 = (s32[189,768]{1,0:T(8,128)S(1)}, s32[189,768]{1,0:T(8,128)}, u32[]{:S(2)}) copy-start(s32[189,768]{1,0:T(8,128)} %param.10) | copy-start | bytes 1741828
  33.8 77.9 %all-to-all-start.1 = ((bf16[128,160,128]{2,1,0:T(8,128)(2,1)}), bf16[128,160,128]{2,1,0:T(8,128)(2,1)}, u32[]{:S(2)}, u32[]{:S(2)}) async-start(bf16[128,160,128]{2,1,0:T(8,128)(2,1)} %shard_map.86), calls=%async_computation.1 | async-start | bytes 10485760 | tf_op jit(solution)/shard_map/all_to_all | solution.py:261

commit v6 on v5

--- a/solution.py
+++ b/solution.py
@@ -11,14 +11,14 @@
 SPLIT = 4
 RING = 3
 ZERO = 8
-PARTS = 8
+PARTS = 4
 LEAF_GROUP = 1
 LEAF_BURST = 9
 LEAF_PIECES = 2
 
 
 def place_far(block, table, base):
-    count = block.shape[0] - LANES // SPLIT
+    count = block.shape[0] * SPLIT // (SPLIT + 1)
     rows, step = count // SPLIT, LANES // SPLIT
     table[pl.ds(base, count, stride=2), :] = block[0:count].astype(jnp.float32)
     rest = block[count:].astype(jnp.float32)
@@ -30,7 +30,7 @@
 def translate_kernel(group, count, scale, packed, burst, pieces, idx_hbm, m2l_ref, *refs):
     near_ref, refs = refs[0], refs[1:]
     if packed:
-        far_hbm, refs = refs[0], refs[1:]
+        far_hbm, refs = refs[0:2], refs[2:]
     out_ref, table, acc, idx_vmem = refs[:4]
     rows_f, kept, smem = refs[4:7], refs[7], refs[8:11]
     sem, vsem = refs[11:13]
@@ -64,14 +64,17 @@
         copy = pltpu.make_async_copy(idx_hbm, idx_vmem, vsem)
         copy.start()
         if packed:
-            far, fsem = refs[13:15]
-            span = far.shape[0] // PARTS
-
-            def part(q):
-                return pltpu.make_async_copy(far_hbm.at[pl.ds(q * span, span)], far.at[pl.ds(q * span, span)], fsem.at[q])
-
-            for q in range(PARTS):
-                part(q).start()
+            far, fsem = refs[13:15], refs[15]
+            span = far[0].shape[0] // PARTS
+            slots = far[0].shape[1] * SPLIT // (SPLIT + 1)
+
+            def part(h, q):
+                place = pl.ds(q * span, span)
+                return pltpu.make_async_copy(far_hbm[h].at[place], far[h].at[place], fsem.at[h, q])
+
+            for h in range(2):
+                for q in range(PARTS):
+                    part(h, q).start()
         acc[...] = jnp.zeros_like(acc)
         last = rows_f[(burst - 1) % RING]
         last[...] = jnp.zeros_like(last)
@@ -87,13 +90,15 @@
         else:
             table[pl.ds(ZERO, n), :] = near_ref[...].astype(jnp.float32)
         if packed:
-            for q in range(PARTS):
-                part(q).wait()
-
-                @pl.loop(0, span)
-                def _(b):
-                    p = q * span + b
-                    place_far(far[p], table, pl.multiple_of(ZERO + n + p * 2 * (far.shape[1] - LANES // SPLIT), 8))
+            for h in range(2):
+                for q in range(PARTS):
+                    part(h, q).wait()
+
+                    @pl.loop(0, span)
+                    def _(b):
+                        p = q * span + b
+                        base = ZERO + n + p * 4 * slots + h * 2 * slots
+                        place_far(far[h][p], table, pl.multiple_of(base, 8))
 
     for c in range(burst):
         k = c % RING
@@ -128,10 +133,10 @@
     ]
     extra = []
     if far is not None:
-        rows += 2 * far.shape[0] * (far.shape[1] - LANES // SPLIT)
-        operands.append(far)
-        in_specs.append(pl.BlockSpec(memory_space=pl.ANY))
-        extra = [pltpu.VMEM(far.shape, far.dtype), pltpu.SemaphoreType.DMA((PARTS,))]
+        rows += 4 * far[0].shape[0] * far[0].shape[1] * SPLIT // (SPLIT + 1)
+        operands += far
+        in_specs += [pl.BlockSpec(memory_space=pl.ANY)] * 2
+        extra = [pltpu.VMEM(x.shape, x.dtype) for x in far] + [pltpu.SemaphoreType.DMA((2, PARTS))]
     return pl.pallas_call(
         functools.partial(translate_kernel, group, count, scale, far is not None, burst, pieces),
         grid=(noff // (burst * group),),
@@ -159,8 +164,7 @@
     table[pl.ds(base + 1, count, stride=2), :] = rest
 
 
-def pick_kernel(capacity, first, idx_ref, cells_ref, *refs):
-    out_ref, table, twice, f0, f1, s0, s1, sem = refs[-8:]
+def pick_kernel(capacity, first, idx_ref, cells_ref, out_ref, table, twice, f0, f1, s0, s1, sem):
     step = pl.program_id(0)
     steps = pl.num_programs(0)
     rows_f, smem = (f0, f1), (s0, s1)
@@ -168,11 +172,11 @@
     rows, lane = capacity // SPLIT, LANES // SPLIT
 
     def fetch(k, s):
-        return pltpu.make_async_copy(twice.at[pl.ds((2 * (first + s) + k) * lines, lines)], smem[k], sem.at[k])
+        return pltpu.make_async_copy(twice.at[pl.ds((2 * s + k) * lines, lines)], smem[k], sem.at[k])
 
     @pl.when(step == 0)
     def _():
-        twice[...] = 2 * idx_ref[...]
+        twice[...] = 2 * idx_ref[:, first:first + capacity]
         for k in range(2):
             fetch(k, 0).start()
         place_cells(cells_ref[...], table, 0)
@@ -195,27 +199,20 @@
             fetch(k, step + 1).start()
 
 
-def pick_rows(cells, chosen, half, partial=None):
-    devices, capacity = chosen.shape
-    lines = 8
-    steps = devices // (4 * lines)
-    first = half * steps
+def pick_rows(cells, chosen, half):
+    devices, capacity = chosen.shape[0], chosen.shape[1] // 2
+    lines = 16
     operands = [chosen, cells]
-    in_specs = [pl.BlockSpec(x.shape, lambda s: (0, 0), pipeline_mode=pl.Buffered(1)) for x in operands]
-    if partial is not None:
-        operands.append(partial)
-        in_specs.append(pl.BlockSpec(memory_space=pl.ANY))
     return pl.pallas_call(
-        functools.partial(pick_kernel, capacity, first),
-        grid=(steps,),
-        in_specs=in_specs,
-        out_specs=pl.BlockSpec((2 * lines, capacity + capacity // SPLIT, LANES), lambda s: (first + s, 0, 0)),
+        functools.partial(pick_kernel, capacity, half * capacity),
+        grid=(devices // (2 * lines),),
+        in_specs=[pl.BlockSpec(x.shape, lambda s: (0, 0), pipeline_mode=pl.Buffered(1)) for x in operands],
+        out_specs=pl.BlockSpec((2 * lines, capacity + capacity // SPLIT, LANES), lambda s: (s, 0, 0)),
         out_shape=jax.ShapeDtypeStruct((devices, capacity + capacity // SPLIT, LANES), jnp.bfloat16),
-        scratch_shapes=[pltpu.VMEM((2 * cells.shape[0], LANES), jnp.float32), pltpu.VMEM(chosen.shape, jnp.int32)]
+        scratch_shapes=[pltpu.VMEM((2 * cells.shape[0], LANES), jnp.float32), pltpu.VMEM((devices, capacity), jnp.int32)]
         + [pltpu.VMEM((2 * lines * capacity, LANES), jnp.float32)] * 2
         + [pltpu.SMEM((lines, capacity), jnp.int32)] * 2
         + [pltpu.SemaphoreType.DMA((2,))],
-        input_output_aliases={} if partial is None else {2: 0},
         compiler_params=pltpu.CompilerParams(vmem_limit_bytes=56 * 2**20),
         cost_estimate=pl.CostEstimate(flops=0, bytes_accessed=24 * 2**20, transcendentals=0),
     )(*operands)
@@ -248,17 +245,19 @@
     ).reshape(narrow * own.shape[0], LANES)
 
     chosen = send_index[0]
-    outgoing = pick_rows(leaf_density, chosen, 0)
-    outgoing, group = lax.optimization_barrier((outgoing, group))
+    one = pick_rows(leaf_density, chosen, 0)
+    one, group = lax.optimization_barrier((one, group))
     up = [(i, i + 1) for i in range(wide - 1)]
     down = [(j, i) for i, j in up]
     before = lax.ppermute(group, "wide", up)
     after = lax.ppermute(group, "wide", down)
-    outgoing = pick_rows(leaf_density, chosen, 1, outgoing)
-    outgoing, before, after, m2l_matrices, leaf_source, coarse_source = lax.optimization_barrier(
-        (outgoing, before, after, m2l_matrices, leaf_source, coarse_source)
+    one, before, after, leaf_later = lax.optimization_barrier((one, before, after, leaf_density))
+    far_one = lax.all_to_all(one, ("wide", "narrow"), split_axis=0, concat_axis=0, tiled=True)
+    two = pick_rows(leaf_later, chosen, 1)
+    two, m2l_matrices, leaf_source, coarse_source = lax.optimization_barrier(
+        (two, m2l_matrices, leaf_source, coarse_source)
     )
-    far = lax.all_to_all(outgoing, ("wide", "narrow"), split_axis=0, concat_axis=0, tiled=True)
+    far_two = lax.all_to_all(two, ("wide", "narrow"), split_axis=0, concat_axis=0, tiled=True)
 
     near = jnp.concatenate([before, group, after], axis=0)
     base = (lax.axis_index("wide") - 1) * (narrow * parents_here)
@@ -270,8 +269,8 @@
     leaf_index = lines_of(
         jnp.where(leaf_source < 0, 0, ZERO + 2 * leaf_source).reshape(noff // LEAF_GROUP, LEAF_GROUP * cells)
     )
-    far, leaf_index, coarse_local = lax.optimization_barrier((far, leaf_index, coarse_local))
-    leaf_local = translate(leaf_index, m2l_matrices, leaf_density, far, LEAF_GROUP, cells, 1, LEAF_BURST, LEAF_PIECES)
+    far_one, far_two, leaf_index, coarse_local = lax.optimization_barrier((far_one, far_two, leaf_index, coarse_local))
+    leaf_local = translate(leaf_index, m2l_matrices, leaf_density, [far_one, far_two], LEAF_GROUP, cells, 1, LEAF_BURST, LEAF_PIECES)
     return (leaf_local, parents, coarse_local)
 
 

time: 226 us -> 260 us (1.15)
  waiting for transfers between devices: 20.5 us -> 32.5 us
  Pallas kernels: 152 us -> 162 us
  starting transfers between devices: 24.7 us -> 31.8 us
  local copies, waits for them, and re-layouts: 25.3 us -> 28.6 us
    pallas_call x2, Pallas kernels: 133 us -> 143 us  [translate(): pl.pallas_call(functools.partial(translate_kernel, group, count, scale, f...]
    ppermute x1, waiting for transfers between devices: 0.01 us -> 6.63 us  [local(): after = lax.ppermute(group, 'wide', down)]
    all_to_all x1 -> x2, starting transfers between devices: 13.2 us -> 19.5 us  [the longest x1 14 us: local(): lax.all_to_all(one, ('wide', 'narrow'), split_axis=0, concat_axis=0, tile...]
    all_to_all x1 -> x2, waiting for transfers between devices: 20.5 us -> 25.7 us  [the longest x1 25.7 us: local(): lax.all_to_all(one, ('wide', 'narrow'), split_axis=0, concat_axis=0, tile...]
    optimization_barrier x1 -> x2, local copies, waits for them, and re-layouts: 21.1 us -> 22.1 us  [the longest x1 21.2 us: local(): lax.optimization_barrier((two, m2l_matrices, leaf_source, coarse_source))]
  transfers between devices with their start and end apart: 4 -> 5, of which waited for: 1 -> 3; matrix products, arithmetic and copies ran while one was open for 11% -> 10% of each run, Pallas kernels for 17% -> 15%
where the time goes in v6:
time: 260 us; the launch traced here: 259 us
  Pallas kernels  162 us (62%)
  waiting for transfers between devices  32.5 us (12%)
  starting transfers between devices  31.8 us (12%)
  local copies, waits for them, and re-layouts  28.6 us (11%)
  other arithmetic  3.29 us (1%)
    pallas_call x2, Pallas kernels, translate(): pl.pallas_call(functools.partial(translate_kernel, group, count, scale, f...  143 us
    all_to_all x1, waiting for transfers between devices, local(): lax.all_to_all(one, ('wide', 'narrow'), split_axis=0, concat_axis=0, tile...  25.7 us
    optimization_barrier x1, local copies, waits for them, and re-layouts, local(): lax.optimization_barrier((two, m2l_matrices, leaf_source, coarse_source))  21.2 us
    pallas_call x2, Pallas kernels, pick_rows(): pl.pallas_call(functools.partial(pick_kernel, capacity, half * capacity),...  18.8 us
    all_to_all x1, starting transfers between devices, local(): lax.all_to_all(one, ('wide', 'narrow'), split_axis=0, concat_axis=0, tile...  14 us
    ppermute x1, waiting for transfers between devices, local(): after = lax.ppermute(group, 'wide', down)  6.63 us
    all_to_all x1, starting transfers between devices, local(): lax.all_to_all(jnp.broadcast_to(own, (narrow,) + own.shape), 'narrow', sp...  5.97 us
    all_to_all x1, starting transfers between devices, local(): lax.all_to_all(two, ('wide', 'narrow'), split_axis=0, concat_axis=0, tile...  5.51 us
  transfers between devices with their start and end apart: 5, of which 3 were waited for; matrix products, arithmetic and copies ran while one was open for 10% of the time, Pallas kernels for 15%

profile of v6, /device:TPU:1, one launch (start us, length us, event | category | flops | bytes accessed | tf_op | source)
XLA Modules:
  0.0 259.1 jit_solution(17774418181074922567)
XLA Ops:
  0.6 0.0 copy-start
  0.6 1.2 copy.14.cells_ref.refs_0_
  1.8 0.0 copy-start.1
  1.8 0.4 reshape.27
  2.2 0.0 copy-done
  2.2 0.4 convolution_convert_fusion
  2.6 0.0 copy-start.8
  2.6 0.1 copy.21
  2.7 0.8 broadcast_in_dim.7
  3.5 6.0 %all-to-all-start = ((bf16[8,192,128]{2,1,0:T(8,128)(2,1)}), bf16[8,192,128]{2,1,0:T(8,128)(2,1)S(1)}, u32[]{:S(2)}, u32[]{:S(2)}) async-start(bf16[8,192,128]{2,1,0:T(8,128)(2,1)} %broadcast_in_dim.7), calls=%async_computation | async-start | bytes 786432 | tf_op jit(solution)/shard_map/all_to_all | solution.py:243
  9.5 0.0 copy-done.1
  9.5 9.4 %shard_map.85 = bf16[128,80,128]{2,1,0:T(8,128)(2,1)} custom-call(s32[128,128]{1,0:T(8,128)} %bitcast.11, bf16[768,152]{1,0:T(8,128)(2,1)} %copy-done.1), custom_call_target="tpu_custom_call" | custom-call | bytes 25165824 | tf_op jit(solution)/shard_map/pallas_call | solution.py:206
  18.9 0.0 all-to-all-done
  18.9 0.0 copy-start.3
  18.9 0.0 copy-start.5
  18.9 1.4 collective-permute-start.1
  20.4 5.0 %collective-permute-start = (bf16[1536,128]{1,0:T(8,128)(2,1)S(1)}, bf16[1536,128]{1,0:T(8,128)(2,1)}, u32[]{:S(2)}, u32[]{:S(2)}) collective-permute-start(bf16[1536,128]{1,0:T(8,128)(2,1)S(1)} %bitcast.9), channel_id=1, source_target_pairs={{0,8},{8,16},{16,24},{24,32},{32,40},{40,48},{48,56},{56,64},{64,7... | collective-permute-start | bytes 1179656 | tf_op jit(solution)/shard_map/ppermute | solution.py:252
  25.3 6.6 %collective-permute-done.1 = bf16[1536,128]{1,0:T(8,128)(2,1)S(1)} collective-permute-done((bf16[1536,128]{1,0:T(8,128)(2,1)S(1)}, bf16[1536,128]{1,0:T(8,128)(2,1)S(1)}, u32[]{:S(2)}, u32[]{:S(2)}) %collective-permute-start.1) | collective-permute-done | bytes 393248 | tf_op jit(solution)/shard_map/ppermute | solution.py:253
  32.0 0.0 copy-start.6
  32.0 0.8 copy-done.6
  32.7 0.2 collective-permute-done
  32.9 0.0 copy-done.3
  32.9 0.0 copy-done.8
  32.9 14.0 %all-to-all-start.1 = ((bf16[128,80,128]{2,1,0:T(8,128)(2,1)}), bf16[128,80,128]{2,1,0:T(8,128)(2,1)S(1)}, u32[]{:S(2)}, u32[]{:S(2)}) async-start(bf16[128,80,128]{2,1,0:T(8,128)(2,1)} %shard_map.85), calls=%async_computation.1 | async-start | bytes 5242880 | tf_op jit(solution)/shard_map/all_to_all | solution.py:255
  46.9 0.0 copy-done.5
  46.9 0.9 copy.17.cells_ref
  47.8 9.5 %shard_map.86 = bf16[128,80,128]{2,1,0:T(8,128)(2,1)} custom-call(s32[128,128]{1,0:T(8,128)} %bitcast.12, bf16[768,152]{1,0:T(8,128)(2,1)} %copy.17.cells_ref), custom_call_target="tpu_custom_call" | custom-call | bytes 25165824 | tf_op jit(solution)/shard_map/pallas_call | solution.py:206
  57.3 0.0 copy-start.9
  57.3 25.7 %all-to-all-done.1.refs_1_ = bf16[128,80,128]{2,1,0:T(8,128)(2,1)S(1)} async-done(((bf16[128,80,128]{2,1,0:T(8,128)(2,1)}), bf16[128,80,128]{2,1,0:T(8,128)(2,1)S(1)}, u32[]{:S(2)}, u32[]{:S(2)}) %all-to-all-start.1) | async-done | bytes 2621472 | tf_op jit(solution)/shard_map/all_to_all | solution.py:255
  83.0 0.0 copy-start.2
  83.0 1.5 copy-done.2
  84.5 5.5 %all-to-all-start.2 = ((bf16[128,80,128]{2,1,0:T(8,128)(2,1)}), bf16[128,80,128]{2,1,0:T(8,128)(2,1)}, u32[]{:S(2)}, u32[]{:S(2)}) async-start(bf16[128,80,128]{2,1,0:T(8,128)(2,1)} %shard_map.86), calls=%async_computation.2 | async-start | bytes 5242880 | tf_op jit(solution)/shard_map/all_to_all | solution.py:260
  90.0 0.0 copy-done.9
  90.0 0.1 reshape.32
  90.1 0.7 reshape.33.idx_hbm
  90.8 1.1 add_select_fusion
  91.9 1.0 reshape.31.idx_hbm
  92.9 0.0 copy-start.4
  92.9 0.0 copy-start.7
  92.9 21.2 %copy.18.m2l_ref = bf16[189,152,152]{2,1,0:T(8,128)(2,1)} copy(bf16[189,152,152]{0,2,1:T(8,128)(2,1)} %param.7) | data formatting | bytes 17466624 | tf_op jit(solution)/shard_map/optimization_barrier | solution.py:257
  114.1 0.0 copy-done.4
  114.1 0.0 copy-done.7
  114.1 2.1 pad_maximum_fusion.refs_0_
  116.2 20.0 %shard_map.87 = f32[152,96]{1,0:T(8,128)} custom-call(s32[21,7,128]{2,1,0:T(8,128)} %reshape.33.idx_hbm, bf16[189,152,152]{2,1,0:T(8,128)(2,1)} %copy.18.m2l_ref, bf16[4608,128]{1,0:T(8,128)(2,1)} %pad_maximum_fusion.refs_0_), custom_call_target="tpu_custom_call" | custom-call | flops 7134511104 | bytes 20971520 | tf_op jit(solution)/shard_map/pallas_call | solution.py:140
  136.3 0.0 all-to-all-done.2.refs_2_
  136.3 122.7 %shard_map.88 = f32[152,768]{1,0:T(8,128)} custom-call(s32[189,6,128]{2,1,0:T(8,128)} %reshape.31.idx_hbm, bf16[189,152,152]{2,1,0:T(8,128)(2,1)} %copy.18.m2l_ref, bf16[768,152]{1,0:T(8,128)(2,1)} %copy-done.1, bf16[128,80,128]{2,1,0:T(8,128)(2,1)} %copy-done.2, bf16[128,80,128]{2,1,0:T(8,128)(2,1)} %all-to-all-done.2.refs_2_), custom_call_target="tpu_custom_call" | custom-call | flops 57076088832 | bytes 20971520 | tf_op jit(solution)/shard_map/pallas_call | solution.py:140
  (4 shorter events, 0.1 us)
Async XLA Ops:
  0.6 1.6 copy-start
  1.8 7.7 %copy-start.1 = (bf16[768,152]{1,0:T(8,128)(2,1)}, bf16[768,152]{1,0:T(8,128)(2,1)S(1)}, u32[]{:S(2)}) copy-start(bf16[768,152]{1,0:T(8,128)(2,1)S(1)} %copy.14.cells_ref.refs_0_) | copy-start | bytes 700420
  2.6 30.3 %copy-start.8 = (bf16[96,152]{0,1:T(8,128)(2,1)}, bf16[96,152]{0,1:T(8,128)(2,1)S(1)}, u32[]{:S(2)}) copy-start(bf16[96,152]{0,1:T(8,128)(2,1)S(1)} %convolution_convert_fusion) | copy-start | bytes 87556
  3.5 15.4 %all-to-all-start = ((bf16[8,192,128]{2,1,0:T(8,128)(2,1)}), bf16[8,192,128]{2,1,0:T(8,128)(2,1)S(1)}, u32[]{:S(2)}, u32[]{:S(2)}) async-start(bf16[8,192,128]{2,1,0:T(8,128)(2,1)} %broadcast_in_dim.7), calls=%async_computation | async-start | bytes 786432 | tf_op jit(solution)/shard_map/all_to_all | solution.py:243
  18.9 14.0 %copy-start.3 = (bf16[8,192,128]{2,1,0:T(8,128)(2,1)}, bf16[8,192,128]{2,1,0:T(8,128)(2,1)S(1)}, u32[]{:S(2)}) copy-start(bf16[8,192,128]{2,1,0:T(8,128)(2,1)S(1)} %all-to-all-done) | copy-start | bytes 1179652
  18.9 28.0 %copy-start.5 = (bf16[768,152]{0,1:T(8,128)(2,1)S(1)}, bf16[768,152]{0,1:T(8,128)(2,1)}, u32[]{:S(2)}) copy-start(bf16[768,152]{0,1:T(8,128)(2,1)} %param.6) | copy-start | bytes 700420
  18.9 13.0 %collective-permute-start.1 = (bf16[1536,128]{1,0:T(8,128)(2,1)S(1)}, bf16[1536,128]{1,0:T(8,128)(2,1)S(1)}, u32[]{:S(2)}, u32[]{:S(2)}) collective-permute-start(bf16[1536,128]{1,0:T(8,128)(2,1)S(1)} %bitcast.8), channel_id=1, source_target_pairs={{8,0},{16,8},{24,16},{32,24},{40,32},{48,40},{56,48},{64,56},{72,6... | collective-permute-start | bytes 1179656 | tf_op jit(solution)/shard_map/ppermute | solution.py:253
  20.4 12.5 %collective-permute-start = (bf16[1536,128]{1,0:T(8,128)(2,1)S(1)}, bf16[1536,128]{1,0:T(8,128)(2,1)}, u32[]{:S(2)}, u32[]{:S(2)}) collective-permute-start(bf16[1536,128]{1,0:T(8,128)(2,1)S(1)} %bitcast.9), channel_id=1, source_target_pairs={{0,8},{8,16},{16,24},{24,32},{32,40},{40,48},{48,56},{56,64},{64,7... | collective-permute-start | bytes 1179656 | tf_op jit(solution)/shard_map/ppermute | solution.py:252
  32.0 0.8 copy-start.6
  32.9 50.1 %all-to-all-start.1 = ((bf16[128,80,128]{2,1,0:T(8,128)(2,1)}), bf16[128,80,128]{2,1,0:T(8,128)(2,1)S(1)}, u32[]{:S(2)}, u32[]{:S(2)}) async-start(bf16[128,80,128]{2,1,0:T(8,128)(2,1)} %shard_map.85), calls=%async_computation.1 | async-start | bytes 5242880 | tf_op jit(solution)/shard_map/all_to_all | solution.py:255
  57.3 32.7 %copy-start.9 = (s32[189,96]{1,0:T(8,128)S(1)}, s32[189,96]{1,0:T(8,128)}, u32[]{:S(2)}) copy-start(s32[189,96]{1,0:T(8,128)} %param.11) | copy-start | bytes 217732
  83.0 1.5 copy-start.2
  84.5 51.8 %all-to-all-start.2 = ((bf16[128,80,128]{2,1,0:T(8,128)(2,1)}), bf16[128,80,128]{2,1,0:T(8,128)(2,1)}, u32[]{:S(2)}, u32[]{:S(2)}) async-start(bf16[128,80,128]{2,1,0:T(8,128)(2,1)} %shard_map.86), calls=%async_computation.2 | async-start | bytes 5242880 | tf_op jit(solution)/shard_map/all_to_all | solution.py:260
  92.9 21.2 %copy-start.4 = (bf16[8,192,128]{2,1,0:T(8,128)(2,1)S(1)}, bf16[8,192,128]{2,1,0:T(8,128)(2,1)}, u32[]{:S(2)}) copy-start(bf16[8,192,128]{2,1,0:T(8,128)(2,1)} %copy-done.3) | copy-start | bytes 1179652
  92.9 21.2 %copy-start.7 = (bf16[1536,128]{1,0:T(8,128)(2,1)S(1)}, bf16[1536,128]{1,0:T(8,128)(2,1)}, u32[]{:S(2)}) copy-start(bf16[1536,128]{1,0:T(8,128)(2,1)} %copy-done.6) | copy-start | bytes 1179652
